TPU v7x, 256 devices: a whole 4x4x8 slice. The times are simulated.
256 devices in a mesh: dp: 32 (over x, y, z_hi), tensor: 8 (over z_lo, core).
Axes of the slice: x: 4, y: 4, z: 8 (z_hi: 2, z_lo: 4; z = z_hi * 4 + z_lo), core: 2. Of those that a mesh axis runs over, the one named last changes fastest.
Arguments:
- tokens: bfloat16 [1024, 16384], P('dp', 'tensor'), may hold values from -6 to 6
- gate_weight: bfloat16 [16384, 28672], P('tensor', 'dp'), may hold values from -0.046875 to 0.046875
- up_weight: bfloat16 [16384, 28672], P('tensor', 'dp'), may hold values from -0.046875 to 0.046875
- down_weight: bfloat16 [28672, 16384], P('dp', 'tensor'), may hold values from -0.03125 to 0.03125
Outputs:
- mixed: bfloat16 [1024, 16384], P('dp', 'tensor')
All inputs are finite; a program needn't handle non-finite values.
Results may differ from a plain program's by a relative error of at most 0.0049.
Values may be sent and summed in bfloat16 or wider, within the bound.
A program may use at most 128 MiB of HBM per device.

v0:
```python
import jax
import jax.numpy as jnp
from jax import lax
from jax.sharding import PartitionSpec as P


def gated_units(sums, width):
    return (jax.nn.silu(sums[:, :width]) * sums[:, width:]).astype(jnp.bfloat16)


def on_device(tokens, gate_weight, up_weight, down_weight):
    width = gate_weight.shape[1]
    piece = lax.all_gather(tokens, "dp", axis=0, tiled=True)
    gate_part = jnp.dot(piece, gate_weight, preferred_element_type=jnp.float32)
    up_part = jnp.dot(piece, up_weight, preferred_element_type=jnp.float32)
    partial_value = jnp.concatenate([gate_part, up_part], axis=1)
    totals = lax.psum(partial_value, "tensor")
    hidden = gated_units(totals, width)
    summed = lax.psum_scatter(
        jnp.dot(hidden, down_weight, preferred_element_type=jnp.float32),
        "dp",
        scatter_dimension=0,
        tiled=True,
    )
    return summed.astype(jnp.bfloat16)


def solution(mesh):
    return jax.shard_map(
        on_device,
        mesh=mesh,
        in_specs=(P("dp", "tensor"), P("tensor", "dp"), P("tensor", "dp"), P("dp", "tensor")),
        out_specs=P("dp", "tensor"),
        check_vma=False,
    )
```

profile of v0, /device:TPU:1, one launch (start us, length us, event | category | flops | bytes accessed | tf_op | source)
XLA Modules:
  0.0 700.1 jit_solution(2614900324405259829)
XLA Ops:
  6.5 0.0 all-gather.2.cloned.1.call-start
  6.5 0.7 all-gather.2.cloned.1.call-update
  7.3 0.0 all-reduce.2.cloned.1.call-start
  7.3 114.8 %all-gather.2.cloned.1.call-done = bf16[1024,2048]{1,0:T(8,128)(2,1)} async-done(((bf16[32,2048]{1,0:T(8,128)(2,1)}), bf16[1024,2048]{1,0:T(8,128)(2,1)}) %all-gather.2.cloned.1.call-update) | async-done | bytes 4194320 | tf_op jit(solution)/shard_map/all_gather | solution.py:13
  122.1 0.0 copy-start
  122.1 0.0 copy-start.1
  122.1 7.1 %fusion.6 = f32[1024,896]{0,1:T(8,128)S(1)} fusion(bf16[1024,2048]{1,0:T(8,128)(2,1)} %all-gather.2.cloned.1.call-done, bf16[2048,896]{1,0:T(8,128)(2,1)} %param.6), kind=kOutput, calls=%fused_computation.7 | convolution fusion | flops 3758096384 | bytes 11534336 | tf_op jit(solution)/shard_map/dot_general | solution.py:15
  129.2 0.0 copy-done
  129.2 0.0 copy-done.1
  129.2 4.2 fusion.5
  133.4 3.7 pad_maximum_fusion
  137.1 0.0 all-reduce.2.cloned.1.call-update
  137.1 0.0 reduce-scatter.2.cloned.1.call-start
  137.1 165.1 %all-reduce.2.cloned.1.call-done = f32[1024,1792]{0,1:T(8,128)} async-done(((f32[1024,1792]{0,1:T(8,128)}), f32[1024,1792]{0,1:T(8,128)}) %all-reduce.2.cloned.1.call-update) | async-done | bytes 7340048 | tf_op jit(solution)/shard_map/psum | solution.py:17
  302.2 12.1 %fusion.1 = f32[1024,2048]{1,0:T(8,128)} fusion(bf16[896,2048]{1,0:T(8,128)(2,1)} %param.7, f32[1024,1792]{0,1:T(8,128)} %all-reduce.2.cloned.1.call-done), kind=kOutput, calls=%fused_computation.3 | convolution fusion | flops 3763601408 | bytes 19398656 | tf_op jit(solution)/shard_map/dot_general | solution.py:20
  314.3 0.0 reduce-scatter.2.cloned.1.call-update
  314.3 377.7 %reduce-scatter.2.cloned.1.call-done = f32[32,2048]{1,0:T(8,128)} async-done(((f32[1024,2048]{1,0:T(8,128)}), f32[32,2048]{1,0:T(8,128)}) %reduce-scatter.2.cloned.1.call-update) | async-done | bytes 262160 | tf_op jit(solution)/shard_map/reduce_scatter | solution.py:19
  692.0 1.6 convert_element_type.7
Async XLA Ops:
  6.5 115.5 %all-gather.2.cloned.1.call-start = ((), (), s32[]{:S(2)}) async-start(), calls=%async_computation.1 | async-start | bytes 4325376 | tf_op jit(solution)/shard_map/all_gather | solution.py:13
  7.3 294.9 %all-reduce.2.cloned.1.call-start = ((), (), s32[]{:S(2)}) async-start(), calls=%async_computation.2 | async-start | bytes 14680064 | tf_op jit(solution)/shard_map/psum | solution.py:17
  122.1 7.1 %copy-start = (bf16[1024,2048]{1,0:T(8,128)(2,1)S(1)}, bf16[1024,2048]{1,0:T(8,128)(2,1)}, u32[]{:S(2)}) copy-start(bf16[1024,2048]{1,0:T(8,128)(2,1)} %all-gather.2.cloned.1.call-done) | copy-start | bytes 12582916
  122.1 7.1 %copy-start.1 = (bf16[2048,896]{1,0:T(8,128)(2,1)S(1)}, bf16[2048,896]{1,0:T(8,128)(2,1)}, u32[]{:S(2)}) copy-start(bf16[2048,896]{1,0:T(8,128)(2,1)} %param.5) | copy-start | bytes 11010052
  137.1 554.9 %reduce-scatter.2.cloned.1.call-start = ((), (), s32[]{:S(2)}) async-start(), calls=%async_computation.3 | async-start | bytes 8650752 | tf_op jit(solution)/shard_map/reduce_scatter | solution.py:19
Sparse Core Ops, SparseCore 0:
  10.8 111.2 all-gather.1
  137.2 164.9 all-reduce.1
  314.4 377.5 reduce-scatter.1
where the time goes:
time: 705 us; the launch traced here: 700 us
  waiting for transfers between devices  658 us (93%)
  matrix products  23.3 us (3%)
  between operations  13.1 us (2%)
    reduce_scatter x1, waiting for transfers between devices, on_device(): lax.psum_scatter(jnp.dot(hidden, down_weight, preferred_element_type=jnp....  378 us
    psum x1, waiting for transfers between devices, on_device(): totals = lax.psum(partial_value, 'tensor')  165 us
    all_gather x1, waiting for transfers between devices, on_device(): piece = lax.all_gather(tokens, 'dp', axis=0, tiled=True)  115 us
  transfers between devices with their start and end apart: 3, of which 3 were waited for; matrix products, arithmetic and copies ran while one was open for 0% of the time, Pallas kernels for 0%

commit v1 on v0

v1 whole, which is shorter than its diff:
```python
import jax
import jax.numpy as jnp
from jax import lax
from jax.experimental import pallas as pl
from jax.experimental.pallas import tpu as pltpu
from jax.sharding import PartitionSpec as P

F32, BF16 = jnp.float32, jnp.bfloat16
CHUNKS = 4
OWN, OTHER, HALF_OF = (0, 3), (1, 2), (0, 0, 1, 1)
SPLIT = ((0, 4), (4, 7))
WIDE = F32


class Sends:
    def __init__(self, send_sem, recv_sem):
        self.send_sem, self.recv_sem = send_sem, recv_sem
        self.ids, self.open = {}, []

    def copy(self, name, src, dst, device):
        number = self.ids.setdefault(name, len(self.ids))
        return pltpu.make_async_remote_copy(
            src_ref=src,
            dst_ref=dst,
            send_sem=self.send_sem.at[number],
            recv_sem=self.recv_sem.at[number],
            device_id=device,
            device_id_type=pl.DeviceIdType.MESH,
        )

    def start(self, name, src, dst, device, when=None):
        one = self.copy(name, src, dst, device)
        one.start()
        self.open.append((one, when))

    def arrived(self, name, dst, device):
        self.copy(name, dst, dst, device).wait_recv()

    def finish(self):
        for one, when in self.open:
            if when is None:
                one.wait_send()
            else:
                pl.when(when)(one.wait_send)


TRANSFERS = 192


def kernel(tokens, gate, up, down, out, tok, wgu, wd, part, pair, zs, zr, hid, mix, s1, r1, t1, r2, t2, z3, local_sem, send_sem, recv_sem):
    dp, tensor = lax.axis_index("dp"), lax.axis_index("tensor")
    x, y, zh = dp // 8, (dp // 2) % 4, dp % 2
    zl, core = tensor // 2, tensor % 2
    pos = jnp.where(core == 0, zl, 3 - zl)
    step = jnp.where(core == 0, 1, -1)

    def plane(dx, dy):
        return ((((x + dx + 4) % 4) * 4 + (y + dy + 4) % 4) * 2 + zh, tensor)

    across = ((x * 4 + y) * 2 + 1 - zh, tensor)
    mate = (dp, zl * 2 + 1 - core)
    ahead = (dp, (zl + step) * 2 + core)
    behind = (dp, (zl - step) * 2 + core)

    mine = [
        pltpu.make_async_copy(tokens.at[pl.ds(16 * h, 16)], tok.at[OWN[h], y, x], local_sem.at[h])
        for h in range(2)
    ]
    weights = []
    for n in range(7):
        for g, ref in enumerate((gate, up)):
            weights.append(
                pltpu.make_async_copy(
                    ref.at[:, pl.ds(128 * n, 128)],
                    wgu.at[:, pl.ds(256 * n + 128 * g, 128)],
                    local_sem.at[2 + 2 * n + g],
                )
            )
    weights.append(pltpu.make_async_copy(down, wd, local_sem.at[16]))
    for one in mine + weights:
        one.start()

    barrier = pltpu.get_barrier_semaphore()

    def greet(device):
        pl.semaphore_signal(barrier, inc=1, device_id=device, device_id_type=pl.DeviceIdType.MESH)

    for dx, dy in ((1, 0), (-1, 0), (2, 0), (0, 1), (0, -1), (0, 2)):
        greet(plane(dx, dy))
    greet(across)
    greet(mate)
    pl.when(pos < 3)(lambda: greet(ahead))
    pl.when(pos > 0)(lambda: greet(behind))
    pl.semaphore_wait(barrier, 8 + jnp.where(pos < 3, 1, 0) + jnp.where(pos > 0, 1, 0))

    net = Sends(send_sem, recv_sem)

    def light(s, d):
        return plane(d, 0) if s == 0 else plane(0, d)

    def heavy(s, d):
        return plane(0, d) if s == 0 else plane(d, 0)

    here = ((y, x), (x, y))

    def at(ref, k, s, a, b):
        cols = pl.ds(1024 * s, 1024)
        return ref.at[k, a, b, :, cols] if s == 0 else ref.at[k, b, a, :, cols]

    every, low, high = pl.ds(0, 4), pl.ds(0, 2), pl.ds(2, 2)

    def tokens_out(h):
        mine[h].wait()
        net.start(("z", h), tok.at[OWN[h], y, x], tok.at[OTHER[h], y, x], across)

    def tokens_light(k):
        if k in OTHER:
            h = HALF_OF[k]
            net.arrived(("z", h), tok.at[k, y, x], across)
        for s in range(2):
            a, b = here[s]
            block = at(tok, k, s, a, b)
            for i, d in enumerate((1, -1, 2)):
                net.start(("light", k, s, i), block, block, light(s, d))

    def tokens_heavy(k, s):
        a, b = here[s]
        for i, d in enumerate((1, -1, 2)):
            net.arrived(("light", k, s, i), at(tok, k, s, a, (b - d + 4) % 4), light(s, d))
        line = at(tok, k, s, a, every)
        for i, d in enumerate((1, -1)):
            net.start(("heavy", k, s, i), line, line, heavy(s, d))

    def tokens_forward(k, s):
        a, b = here[s]
        for i, (d, half) in enumerate(((1, low), (-1, high))):
            net.arrived(("heavy", k, s, i), at(tok, k, s, (a - d + 4) % 4, every), heavy(s, d))
            block = at(tok, k, s, (a - d + 4) % 4, half)
            net.start(("forward", k, s, i), block, block, heavy(s, d))

    def tokens_in(k):
        for s in range(2):
            a, b = here[s]
            for i, (d, half) in enumerate(((1, low), (-1, high))):
                net.arrived(("forward", k, s, i), at(tok, k, s, (a + 2) % 4, half), heavy(s, d))

    def columns(j):
        return pl.ds(256 * SPLIT[j][0], 256 * (SPLIT[j][1] - SPLIT[j][0]))

    def units(j):
        return pl.ds(128 * SPLIT[j][0], 128 * (SPLIT[j][1] - SPLIT[j][0]))

    def multiply(k, j):
        if k == 0:
            for one in weights[2 * SPLIT[j][0] : 2 * SPLIT[j][1]]:
                one.wait()

        @pl.loop(*SPLIT[j])
        def _(n):
            cols = pl.ds(pl.multiple_of(n * 256, 256), 256)
            value = jnp.dot(tok[k].reshape(256, 2048), wgu[:, cols], preferred_element_type=F32)
            part[k, :, :, cols] = value.reshape(2, 128, 256)

        net.start(("pair", k, j), part.at[k, 1 - core, :, columns(j)], pair.at[k, :, columns(j)], mate)

    def total(k, j, rows, more):
        cols = columns(j)
        value = part[k, core, rows, cols] + pair[k, rows, cols]
        if more:
            value = value + zr[k, rows, cols].astype(F32)
        return value

    def pass_on(k, j, more):
        @pl.loop(0, 8)
        def _(r):
            rows = pl.ds(pl.multiple_of(r * 16, 16), 16)
            zs[k, rows, columns(j)] = total(k, j, rows, more).astype(BF16)

        net.start(("line", k, j), zs.at[k, :, columns(j)], zr.at[k, :, columns(j)], ahead, pos < 3)

    def line_in(k, j):
        net.arrived(("line", k, j), zr.at[k, :, columns(j)], behind)

    def line(k, j, p):
        if p == 0:
            net.arrived(("pair", k, j), pair.at[k, :, columns(j)], mate)

        def go():
            if p:
                line_in(k, j)
            if p < 3:
                pass_on(k, j, p > 0)
            else:
                activate(k, j)

        kept = net.open[:]
        pl.when(pos == p)(go)
        net.open = kept

    def block_of(k, j):
        return hid.at[k, core, :, units(j)]

    def share(k, j):
        net.start(("share", k, j), block_of(k, j), block_of(k, j), mate)

    def hand_back(k, j):
        net.start(("back", k, j), block_of(k, j), block_of(k, j), behind)

    def activate(k, j):
        @pl.loop(0, 8)
        def _(r):
            rows = pl.ds(pl.multiple_of(r * 16, 16), 16)
            value = total(k, j, rows, True)
            for n in range(SPLIT[j][1] - SPLIT[j][0]):
                g, u = value[:, 256 * n : 256 * n + 128], value[:, 256 * n + 128 : 256 * n + 256]
                unit = 128 * (SPLIT[j][0] + n)
                hid[k, core, rows, unit : unit + 128] = (g / (1.0 + jnp.exp(-g)) * u).astype(BF16)

        hand_back(k, j)
        share(k, j)

    def back(k, j, p):
        def go():
            net.arrived(("back", k, j), block_of(k, j), ahead)
            if p > 0:
                hand_back(k, j)
            share(k, j)

        kept = net.open[:]
        pl.when(pos == p)(go)
        net.open = kept

    def project(k, s):
        if s == 0:
            if k == 0:
                weights[14].wait()
            for j in range(2):
                net.arrived(("share", k, j), hid.at[k, 1 - core, :, units(j)], mate)

        @pl.loop(4 * s, 4 * s + 4)
        def _(n):
            cols = pl.ds(pl.multiple_of(n * 256, 256), 256)
            value = jnp.dot(hid[k].reshape(256, 896), wd[:, cols], preferred_element_type=F32)
            mix[k, :, :, :, cols] = value.reshape(4, 4, 16, 256)

        a, b = here[s]
        for m, (to, d, half) in enumerate(((2, 1, low), (2, -1, high), (1, 1, high), (-1, -1, low))):
            s1[k, s, m] = at(mix, k, s, (a + to + 4) % 4, half)[...].astype(BF16)
            net.start(("first", k, s, m), s1.at[k, s, m], r1.at[k, s, m], heavy(s, d))

    def scatter_sum(k, s):
        a, b = here[s]
        for m, (d, half) in enumerate(((1, low), (-1, high))):
            net.arrived(("first", k, s, m), r1.at[k, s, m], heavy(s, d))
            value = at(mix, k, s, (a + d + 4) % 4, half)[...] + r1[k, s, m].astype(F32)
            s1[k, s, 4 + m] = value.astype(BF16)
            net.start(("first", k, s, 4 + m), s1.at[k, s, 4 + m], r1.at[k, s, 4 + m], heavy(s, d))

    def scatter_light(k, s):
        a, b = here[s]
        for m in (2, 3, 4, 5):
            net.arrived(("first", k, s, m), r1.at[k, s, m], heavy(s, 1))
        for half, (m, n) in ((0, (4, 3)), (1, (2, 5))):
            own = at(mix, k, s, a, (low, high)[half])[...]
            t1[k, s, 2 * half : 2 * half + 2] = own + r1[k, s, m].astype(F32) + r1[k, s, n].astype(F32)
        for i, d in enumerate((1, -1, 2)):
            net.start(("second", k, s, i), t1.at[k, s, (b + d + 4) % 4], r2.at[k, s, i], light(s, d))

    def scatter_across(k, s):
        a, b = here[s]
        value = t1[k, s, b]
        for i in range(3):
            net.arrived(("second", k, s, i), r2.at[k, s, i], light(s, 1))
            value = value + r2[k, s, i]
        h = HALF_OF[k]
        if k in OTHER:
            t2[h, s] = value
            net.start(("third", h, s), t2.at[h, s], z3.at[h, s], across)
        else:
            net.arrived(("third", h, s), z3.at[h, s], across)
            out[16 * h : 16 * h + 16, 1024 * s : 1024 * s + 1024] = (value + z3[h, s]).astype(BF16)

    tasks = []

    def task(time, fn, *args):
        tasks.append((time, len(tasks), fn, args))

    for h in range(2):
        task(0, tokens_out, h)
    for k in range(CHUNKS):
        begin = (0.1, 3, 8, 13)[k]
        task(begin, tokens_light, k)
        for s in range(2):
            task(begin + 3.5, tokens_heavy, k, s)
            task(begin + 7, tokens_forward, k, s)
        ready = begin + 11
        for j in range(2):
            task(ready + 0.1 + 1.5 * j, multiply, k, j)
            piece = 14 + 3.5 * (2 * k + j)
            for p in range(4):
                task(piece + 4.5 * p, line, k, j, p)
            for p in (2, 1, 0):
                task(piece + 13.5 + 4 * (3 - p), back, k, j, p)
        task(ready, tokens_in, k)
        done = 14 + 3.5 * (2 * k + 1) + 28
        for s in range(2):
            task(done + 1 * s, project, k, s)
            task(done + 4 + 0.5 * s, scatter_sum, k, s)
            task(done + 8 + 0.5 * s, scatter_light, k, s)
            task(done + 12 + 0.5 * s + (10 if k == 0 else 0), scatter_across, k, s)
    for _, _, fn, args in sorted(tasks, key=lambda t: t[:2]):
        fn(*args)

    for k in range(CHUNKS):
        for j in range(2):
            lined = net.copy(("line", k, j), zs.at[k, :, columns(j)], zr.at[k, :, columns(j)], ahead)
            pl.when(pos < 3)(lined.wait_send)
            backed = net.copy(("back", k, j), block_of(k, j), block_of(k, j), behind)
            pl.when(pos > 0)(backed.wait_send)
            net.copy(("share", k, j), block_of(k, j), block_of(k, j), mate).wait_send()
    net.finish()


def on_device(tokens, gate_weight, up_weight, down_weight):
    hbm = pl.BlockSpec(memory_space=pl.ANY)
    n = CHUNKS
    return pl.pallas_call(
        kernel,
        out_shape=jax.ShapeDtypeStruct((32, 2048), BF16),
        in_specs=[hbm] * 4,
        out_specs=pl.BlockSpec(memory_space=pltpu.VMEM),
        scratch_shapes=[
            pltpu.VMEM((n, 4, 4, 16, 2048), BF16),
            pltpu.VMEM((2048, 1792), BF16),
            pltpu.VMEM((896, 2048), BF16),
            pltpu.VMEM((n, 2, 128, 1792), F32),
            pltpu.VMEM((n, 128, 1792), F32),
            pltpu.VMEM((n, 128, 1792), BF16),
            pltpu.VMEM((n, 128, 1792), BF16),
            pltpu.VMEM((n, 2, 128, 896), BF16),
            pltpu.VMEM((n, 4, 4, 16, 2048), F32),
            pltpu.VMEM((n, 2, 6, 2, 16, 1024), BF16),
            pltpu.VMEM((n, 2, 6, 2, 16, 1024), BF16),
            pltpu.VMEM((n, 2, 4, 16, 1024), WIDE),
            pltpu.VMEM((n, 2, 3, 16, 1024), WIDE),
            pltpu.VMEM((2, 2, 16, 1024), F32),
            pltpu.VMEM((2, 2, 16, 1024), F32),
            pltpu.SemaphoreType.DMA((17,)),
            pltpu.SemaphoreType.DMA((TRANSFERS,)),
            pltpu.SemaphoreType.DMA((TRANSFERS,)),
        ],
        compiler_params=pltpu.CompilerParams(
            collective_id=0, has_side_effects=True, vmem_limit_bytes=60 * 2**20
        ),
        name="panel",
    )(tokens, gate_weight, up_weight, down_weight)


def solution(mesh):
    return jax.shard_map(
        on_device,
        mesh=mesh,
        in_specs=(P("dp", "tensor"), P("tensor", "dp"), P("tensor", "dp"), P("dp", "tensor")),
        out_specs=P("dp", "tensor"),
        check_vma=False,
    )
```

time: 705 us -> 122 us (0.17)
  the two profiles are of different devices: /device:TPU:1 before, /device:TPU:8 now
where the time goes in v1:
time: 122 us
  Pallas kernels  120 us (98%)
  local copies, waits for them, and re-layouts  1.57 us (1%)
    pallas_call x1, Pallas kernels, on_device(): pl.pallas_call(kernel, out_shape=jax.ShapeDtypeStruct((32, 2048), BF16),...  120 us

profile of v1, /device:TPU:8, one launch (start us, length us, event | category | flops | bytes accessed | tf_op | source)
XLA Modules:
  0.0 121.8 jit_solution(7248549808769394056)
XLA Ops:
  0.0 120.2 %panel.1 = bf16[32,2048]{1,0:T(8,128)(2,1)} custom-call(bf16[32,2048]{1,0:T(8,128)(2,1)} %tokens.1, bf16[2048,896]{1,0:T(8,128)(2,1)} %gate.1, bf16[2048,896]{1,0:T(8,128)(2,1)} %up.1, bf16[896,2048]{1,0:T(8,128)(2,1)} %down.1), custom_call_target="tpu_custom_call" | custom-call | tf_op jit(solution)/shard_map/panel/pallas_call | solution.py:327
  120.2 1.6 %copy.6 = bf16[32,2048]{1,0:T(8,128)(2,1)} copy(bf16[32,2048]{1,0:T(8,128)(2,1)} %panel.1) | data formatting | bytes 262144

commit v2 on v1

v2 whole, which is shorter than its diff:
```python
import jax
import jax.numpy as jnp
from jax import lax
from jax.experimental import pallas as pl
from jax.experimental.pallas import tpu as pltpu
from jax.sharding import PartitionSpec as P

F32, BF16 = jnp.float32, jnp.bfloat16
CHUNKS = 4
OWN, OTHER, HALF_OF = (0, 3), (1, 2), (0, 0, 1, 1)
SPLIT = ((0, 2), (2, 4), (4, 6), (6, 7))
MEET = ((1, 1, 1, 1), (1, 1, 1, 1), (1, 1, 1, 1), (1, 1, 1, 1))
GATHER_DIRECT = (1, 1, 1, 1)
SCATTER_DIRECT = (1, 1, 1, 1)
SECOND, THIRD = BF16, BF16
POOL = 48
PIECES = len(SPLIT)

ORDER = (
    (0, 0), (1, 0), (0, 1), (1, 3), (2, 0, 0), (2, 0, 1), (1, 1), (1, 2), (2, 3, 1), (2, 3, 0), (4, 0),
    (5, 0, 1), (5, 0, 0), (6, 0, 1, 0), (5, 0, 2), (2, 1, 0), (6, 0, 0, 0), (2, 1, 1), (6, 0, 2, 0), (5, 0, 3),
    (6, 0, 1, 1), (4, 3), (5, 3, 0), (5, 3, 3), (2, 2, 0), (6, 0, 3, 0), (2, 2, 1), (5, 3, 1), (6, 0, 2, 1),
    (6, 3, 0, 0), (5, 3, 2), (6, 0, 3, 1), (6, 3, 1, 0), (4, 1), (5, 1, 0), (6, 0, 0, 1), (6, 3, 3, 0),
    (5, 1, 2), (5, 1, 1), (6, 0, 1, 2), (7, 0, 1, 3), (6, 3, 2, 0), (6, 1, 0, 0), (6, 3, 0, 1), (5, 1, 3),
    (4, 2), (5, 2, 1), (6, 3, 1, 1), (6, 0, 2, 2), (6, 0, 0, 2), (6, 0, 3, 2), (5, 2, 3), (6, 1, 1, 0),
    (6, 3, 0, 2), (7, 0, 0, 3), (6, 3, 3, 1), (5, 2, 0), (6, 1, 3, 0), (6, 3, 1, 2), (6, 1, 2, 0), (5, 2, 2),
    (7, 0, 0, 1), (7, 0, 3, 1), (7, 0, 2, 1), (7, 0, 1, 1), (7, 0, 1, 0), (7, 0, 3, 0), (6, 3, 2, 1),
    (7, 3, 0, 1), (7, 3, 0, 0), (7, 0, 3, 3), (6, 1, 0, 1), (7, 0, 0, 0), (7, 0, 2, 0), (7, 0, 2, 3),
    (8, 0, 0), (6, 1, 1, 1), (6, 1, 3, 1), (6, 3, 3, 2), (7, 3, 3, 3), (6, 3, 2, 2), (7, 3, 2, 1),
    (6, 1, 0, 2), (7, 3, 1, 1), (6, 2, 0, 0), (6, 1, 2, 1), (8, 0, 1), (7, 3, 0, 3), (6, 2, 2, 0),
    (6, 2, 3, 0), (6, 2, 1, 0), (7, 3, 2, 0), (7, 3, 2, 3), (6, 1, 1, 2), (7, 3, 1, 3), (7, 3, 3, 1),
    (6, 1, 3, 2), (7, 3, 3, 0), (6, 1, 2, 2), (7, 3, 1, 0), (7, 1, 0, 1), (7, 1, 0, 0), (8, 3, 0),
    (6, 2, 0, 1), (6, 2, 3, 1), (6, 2, 2, 1), (7, 1, 1, 3), (8, 3, 1), (7, 1, 1, 1), (7, 1, 2, 3),
    (7, 1, 1, 0), (7, 1, 3, 1), (7, 1, 0, 3), (6, 2, 1, 1), (6, 2, 0, 2), (10, 0, 1), (6, 2, 3, 2),
    (6, 2, 2, 2), (7, 1, 3, 3), (7, 2, 3, 3), (6, 2, 1, 2), (7, 2, 2, 3), (7, 1, 2, 1), (7, 1, 2, 0),
    (7, 1, 3, 0), (7, 2, 0, 3), (8, 1, 0), (7, 2, 1, 3), (8, 1, 1), (7, 2, 3, 1), (7, 2, 3, 0), (7, 2, 0, 1),
    (7, 2, 2, 1), (7, 2, 0, 0), (7, 2, 2, 0), (7, 2, 1, 1), (7, 2, 1, 0), (8, 2, 0), (10, 1, 0), (8, 2, 1),
    (10, 1, 1), (10, 2, 0), (10, 3, 0), (11, 1, 0), (11, 1, 1), (10, 0, 0), (10, 2, 1), (11, 2, 0), (11, 2, 1),
    (10, 3, 1), (11, 0, 1), (11, 3, 0), (11, 0, 0), (11, 3, 1),
)


class Net:
    def __init__(self, send_sem, recv_sem):
        self.send_sem, self.recv_sem = send_sem, recv_sem
        self.arrivals, self.free, self.slots = {}, [], 0

    def take(self):
        if self.slots < POOL:
            self.slots += 1
            return self.slots - 1
        slot, one, when = self.free.pop(0)
        self.wait(one, when)
        return slot

    def give(self, slot, one, when=None):
        self.free.append((slot, one, when))

    def wait(self, one, when):
        if when is None:
            one.wait_send()
        else:
            pl.when(when)(one.wait_send)

    def copy(self, slot, name, src, dst, device):
        number = self.arrivals.setdefault(name, len(self.arrivals))
        return pltpu.make_async_remote_copy(
            src_ref=src,
            dst_ref=dst,
            send_sem=self.send_sem.at[slot],
            recv_sem=self.recv_sem.at[number],
            device_id=device,
            device_id_type=pl.DeviceIdType.MESH,
        )

    def start(self, name, src, dst, device):
        slot = self.take()
        one = self.copy(slot, name, src, dst, device)
        one.start()
        self.give(slot, one)

    def arrived(self, name, dst, device):
        assert name in self.arrivals
        self.copy(0, name, dst, dst, device).wait_recv()

    def finish(self):
        for _, one, when in self.free:
            self.wait(one, when)


ARRIVALS = 132


def kernel(tokens, gate, up, down, out, tok, wgu, wd, part, pair, zs, zr, hid, mix, s1, r1, t1, t1s, r2, t2, z3, local_sem, send_sem, recv_sem):
    dp, tensor = lax.axis_index("dp"), lax.axis_index("tensor")
    x, y, zh = dp // 8, (dp // 2) % 4, dp % 2
    zl, core = tensor // 2, tensor % 2
    pos = jnp.where(core == 0, zl, 3 - zl)
    step = jnp.where(core == 0, 1, -1)

    def plane(dx, dy):
        return ((((x + dx + 4) % 4) * 4 + (y + dy + 4) % 4) * 2 + zh, tensor)

    across = ((x * 4 + y) * 2 + 1 - zh, tensor)
    mate = (dp, zl * 2 + 1 - core)
    ahead = (dp, (zl + step) * 2 + core)
    behind = (dp, (zl - step) * 2 + core)

    def columns(j):
        return pl.ds(256 * SPLIT[j][0], 256 * (SPLIT[j][1] - SPLIT[j][0]))

    def units(j):
        return pl.ds(128 * SPLIT[j][0], 128 * (SPLIT[j][1] - SPLIT[j][0]))

    mine = [
        pltpu.make_async_copy(tokens.at[pl.ds(16 * h, 16)], tok.at[OWN[h], y, x], local_sem.at[h])
        for h in range(2)
    ]
    for one in mine:
        one.start()
    for j in range(PIECES):
        for n in range(*SPLIT[j]):
            for g, ref in enumerate((gate, up)):
                pltpu.make_async_copy(
                    ref.at[:, pl.ds(128 * n, 128)],
                    wgu.at[:, pl.ds(256 * n + 128 * g, 128)],
                    local_sem.at[2 + j],
                ).start()
    weights = [
        pltpu.make_async_copy(wgu.at[:, columns(j)], wgu.at[:, columns(j)], local_sem.at[2 + j])
        for j in range(PIECES)
    ]
    weights.append(pltpu.make_async_copy(down, wd, local_sem.at[2 + PIECES]))
    weights[-1].start()
    unread = set(range(PIECES + 1))

    def weight(j):
        if j in unread:
            unread.remove(j)
            weights[j].wait()

    barrier = pltpu.get_barrier_semaphore()

    def greet(device):
        pl.semaphore_signal(barrier, inc=1, device_id=device, device_id_type=pl.DeviceIdType.MESH)

    for dx, dy in ((1, 0), (-1, 0), (2, 0), (0, 1), (0, -1), (0, 2)):
        greet(plane(dx, dy))
    greet(across)
    greet(mate)
    pl.when(pos < 3)(lambda: greet(ahead))
    pl.when(pos > 0)(lambda: greet(behind))
    pl.semaphore_wait(barrier, 8 + jnp.where(pos < 3, 1, 0) + jnp.where(pos > 0, 1, 0))

    net = Net(send_sem, recv_sem)

    def light(s, d):
        return plane(d, 0) if s == 0 else plane(0, d)

    def heavy(s, d):
        return plane(0, d) if s == 0 else plane(d, 0)

    here = ((y, x), (x, y))

    def at(ref, k, s, a, b):
        cols = pl.ds(1024 * s, 1024)
        return ref.at[k, a, b, :, cols] if s == 0 else ref.at[k, b, a, :, cols]

    every, low, high, three = pl.ds(0, 4), pl.ds(0, 2), pl.ds(2, 2), pl.ds(0, 3)

    def tokens_out(h):
        mine[h].wait()
        net.start(("z", h), tok.at[OWN[h], y, x], tok.at[OTHER[h], y, x], across)

    def tokens_light(k):
        if k in OTHER:
            net.arrived(("z", HALF_OF[k]), tok.at[k, y, x], across)
        for s in range(2):
            a, b = here[s]
            block = at(tok, k, s, a, b)
            for d in (1, -1, 2):
                net.start(("light", k, s), block, block, light(s, d))

    def tokens_heavy(k, s):
        a, b = here[s]
        net.arrived(("light", k, s), at(tok, k, s, a, three), light(s, 1))
        line = at(tok, k, s, a, every)
        for d in (1, -1, 2) if GATHER_DIRECT[k] else (1, -1):
            net.start(("heavy", k, s), line, line, heavy(s, d))

    def tokens_forward(k, s):
        a, b = here[s]
        net.arrived(("heavy", k, s), at(tok, k, s, low, every), heavy(s, 1))
        for d, half in ((1, low), (-1, high)):
            block = at(tok, k, s, (a - d + 4) % 4, half)
            net.start(("forward", k, s), block, block, heavy(s, d))

    def tokens_in(k):
        for s in range(2):
            if GATHER_DIRECT[k]:
                net.arrived(("heavy", k, s), at(tok, k, s, three, every), heavy(s, 1))
            else:
                net.arrived(("forward", k, s), at(tok, k, s, 0, every), heavy(s, 1))

    def multiply(k, j):
        weight(j)

        @pl.loop(*SPLIT[j])
        def _(n):
            cols = pl.ds(pl.multiple_of(n * 256, 256), 256)
            value = jnp.dot(tok[k].reshape(256, 2048), wgu[:, cols], preferred_element_type=F32)
            part[k, :, :, cols] = value.reshape(2, 128, 256)

        net.start(("pair", k, j), part.at[k, 1 - core, :, columns(j)], pair.at[k, :, columns(j)], mate)

    def total(k, j, rows, *more):
        cols = columns(j)
        value = part[k, core, rows, cols] + pair[k, rows, cols]
        for ref in more:
            value = value + ref[k, rows, cols].astype(F32)
        return value

    held = {}

    def end(k, j):
        return 2 if MEET[k][j] else 3

    def line_copy(k, j, up):
        src = zs.at[k, :, columns(j)]
        if up:
            return net.copy(held["line", k, j], ("line", k, j), src, zr.at[k, :, columns(j)], ahead)
        return net.copy(held["line", k, j], ("down", k, j), src, src, behind)

    def pass_on(k, j, up, *more):
        @pl.loop(0, 8)
        def _(r):
            rows = pl.ds(pl.multiple_of(r * 16, 16), 16)
            zs[k, rows, columns(j)] = total(k, j, rows, *more).astype(BF16)

        line_copy(k, j, up).start()

    def hidden_copy(k, j, name):
        block = hid.at[k, core, :, units(j)]
        arrival = ("share", k) if name == "share" else ("back", k, j)
        device = {"share": mate, "back": behind, "onward": ahead}[name]
        return net.copy(held[name, k, j], arrival, block, block, device)

    def hidden_out(k, j, *names):
        for name in names:
            hidden_copy(k, j, name).start()

    def activate(k, j, *more):
        @pl.loop(0, 8)
        def _(r):
            rows = pl.ds(pl.multiple_of(r * 16, 16), 16)
            value = total(k, j, rows, *more)
            for n in range(SPLIT[j][1] - SPLIT[j][0]):
                g, u = value[:, 256 * n : 256 * n + 128], value[:, 256 * n + 128 : 256 * n + 256]
                unit = 128 * (SPLIT[j][0] + n)
                hid[k, core, rows, unit : unit + 128] = (g / (1.0 + jnp.exp(-g)) * u).astype(BF16)

    def line(k, j, p):
        if p == 0:
            held["line", k, j] = net.take()
            net.arrived(("pair", k, j), pair.at[k, :, columns(j)], mate)
        if p == end(k, j):
            for name in ("back", "share") + (("onward",) if MEET[k][j] else ()):
                held[name, k, j] = net.take()

        def go():
            if p == 0:
                pass_on(k, j, True)
                return
            net.arrived(("line", k, j), zr.at[k, :, columns(j)], behind)
            if p < end(k, j):
                pass_on(k, j, True, zr)
            elif MEET[k][j]:
                net.arrived(("down", k, j), zs.at[k, :, columns(j)], ahead)
                activate(k, j, zr, zs)
                hidden_out(k, j, "back", "onward", "share")
            else:
                activate(k, j, zr)
                hidden_out(k, j, "back", "share")

        pl.when(pos == p)(go)
        if p == 0 and MEET[k][j]:
            pl.when(pos == 3)(lambda: pass_on(k, j, False))
        if p == end(k, j) - 1:
            net.give(held["line", k, j], line_copy(k, j, True), pos != end(k, j))

    backs = {}

    def back(k, j, p):
        def go():
            net.arrived(("back", k, j), hid.at[k, core, :, units(j)], ahead if p < end(k, j) else behind)
            hidden_out(k, j, *(("back",) if p and p < end(k, j) else ()), "share")

        pl.when(pos == p)(go)
        backs[k, j] = backs.get((k, j), 0) + 1
        if backs[k, j] == 3:
            senders = (pos == 1) | (pos == 2) if MEET[k][j] else pos > 0
            net.give(held["back", k, j], hidden_copy(k, j, "back"), senders)
            net.give(held["share", k, j], hidden_copy(k, j, "share"))
            if MEET[k][j]:
                net.give(held["onward", k, j], hidden_copy(k, j, "onward"), pos == 2)

    def project(k, s):
        if s == 0:
            weight(PIECES)
            net.arrived(("share", k), hid.at[k, 1 - core], mate)

        @pl.loop(4 * s, 4 * s + 4)
        def _(n):
            cols = pl.ds(pl.multiple_of(n * 256, 256), 256)
            value = jnp.dot(hid[k].reshape(256, 896), wd[:, cols], preferred_element_type=F32)
            mix[k, :, :, :, cols] = value.reshape(4, 4, 16, 256)

        a, b = here[s]
        if SCATTER_DIRECT[k]:
            for i, d in enumerate((1, -1, 2)):
                s1[k, s, i] = at(mix, k, s, (a + d + 4) % 4, every)[...].astype(BF16)
                net.start(("last", k, s), s1.at[k, s, i], r1.at[k, s, i], heavy(s, d))
            return
        sends = ((0, low, 2, 1, low), (0, high, 2, -1, high), (1, high, 1, 1, high), (2, low, -1, -1, low))
        for i, place, to, d, half in sends:
            s1[k, s, i, place] = at(mix, k, s, (a + to + 4) % 4, half)[...].astype(BF16)
            name = "first" if i == 0 else "last"
            net.start((name, k, s), s1.at[k, s, i, place], r1.at[k, s, i, place], heavy(s, d))

    def scatter_sum(k, s):
        a, b = here[s]
        net.arrived(("first", k, s), r1.at[k, s, 0], heavy(s, 1))
        for i, half, d in ((1, low, 1), (2, high, -1)):
            value = at(mix, k, s, (a + d + 4) % 4, half)[...] + r1[k, s, 0, half].astype(F32)
            s1[k, s, i, half] = value.astype(BF16)
            net.start(("last", k, s), s1.at[k, s, i, half], r1.at[k, s, i, half], heavy(s, d))

    def scatter_light(k, s):
        a, b = here[s]
        value = at(mix, k, s, a, every)[...]
        if SCATTER_DIRECT[k]:
            net.arrived(("last", k, s), r1.at[k, s], heavy(s, 1))
            value = value + r1[k, s, 0].astype(F32)
        else:
            net.arrived(("last", k, s), r1.at[k, s, pl.ds(1, 2)], heavy(s, 1))
        value = value + r1[k, s, 1].astype(F32) + r1[k, s, 2].astype(F32)
        t1[k, s] = value
        t1s[k, s] = value.astype(SECOND)
        for i, d in enumerate((1, -1, 2)):
            net.start(("second", k, s), t1s.at[k, s, (b + d + 4) % 4], r2.at[k, s, i], light(s, d))

    def scatter_across(k, s):
        a, b = here[s]
        net.arrived(("second", k, s), r2.at[k, s], light(s, 1))
        value = t1[k, s, b]
        for i in range(3):
            value = value + r2[k, s, i].astype(F32)
        h = HALF_OF[k]
        if k in OTHER:
            t2[h, s] = value.astype(THIRD)
            net.start(("third", h, s), t2.at[h, s], z3.at[h, s], across)
        else:
            net.arrived(("third", h, s), z3.at[h, s], across)
            out[16 * h : 16 * h + 16, 1024 * s : 1024 * s + 1024] = (value + z3[h, s].astype(F32)).astype(BF16)

    STEPS = (
        tokens_out, tokens_light, tokens_heavy, tokens_forward, tokens_in, multiply,
        line, back, project, scatter_sum, scatter_light, scatter_across,
    )
    for number, *args in ORDER:
        STEPS[number](*args)
    net.finish()


def on_device(tokens, gate_weight, up_weight, down_weight):
    hbm = pl.BlockSpec(memory_space=pl.ANY)
    n = CHUNKS
    return pl.pallas_call(
        kernel,
        out_shape=jax.ShapeDtypeStruct((32, 2048), BF16),
        in_specs=[hbm] * 4,
        out_specs=pl.BlockSpec(memory_space=pltpu.VMEM),
        scratch_shapes=[
            pltpu.VMEM((n, 4, 4, 16, 2048), BF16),
            pltpu.VMEM((2048, 1792), BF16),
            pltpu.VMEM((896, 2048), BF16),
            pltpu.VMEM((n, 2, 128, 1792), F32),
            pltpu.VMEM((n, 128, 1792), F32),
            pltpu.VMEM((n, 128, 1792), BF16),
            pltpu.VMEM((n, 128, 1792), BF16),
            pltpu.VMEM((n, 2, 128, 896), BF16),
            pltpu.VMEM((n, 4, 4, 16, 2048), F32),
            pltpu.VMEM((n, 2, 3, 4, 16, 1024), BF16),
            pltpu.VMEM((n, 2, 3, 4, 16, 1024), BF16),
            pltpu.VMEM((n, 2, 4, 16, 1024), F32),
            pltpu.VMEM((n, 2, 4, 16, 1024), SECOND),
            pltpu.VMEM((n, 2, 3, 16, 1024), SECOND),
            pltpu.VMEM((2, 2, 16, 1024), THIRD),
            pltpu.VMEM((2, 2, 16, 1024), THIRD),
            pltpu.SemaphoreType.DMA((3 + PIECES,)),
            pltpu.SemaphoreType.DMA((POOL,)),
            pltpu.SemaphoreType.DMA((ARRIVALS,)),
        ],
        compiler_params=pltpu.CompilerParams(
            collective_id=0, has_side_effects=True, vmem_limit_bytes=60 * 2**20
        ),
        name="panel",
    )(tokens, gate_weight, up_weight, down_weight)


def solution(mesh):
    return jax.shard_map(
        on_device,
        mesh=mesh,
        in_specs=(P("dp", "tensor"), P("tensor", "dp"), P("tensor", "dp"), P("dp", "tensor")),
        out_specs=P("dp", "tensor"),
        check_vma=False,
    )
```

time: 122 us -> 104 us (0.85)
  the two profiles are of different devices: /device:TPU:8 before, /device:TPU:1 now
where the time goes in v2:
time: 104 us
  Pallas kernels  102 us (98%)
  local copies, waits for them, and re-layouts  1.57 us (2%)
    pallas_call x1, Pallas kernels, on_device(): pl.pallas_call(kernel, out_shape=jax.ShapeDtypeStruct((32, 2048), BF16),...  102 us

profile of v2, /device:TPU:1, one launch (start us, length us, event | category | flops | bytes accessed | tf_op | source)
XLA Modules:
  0.0 103.7 jit_solution(7275210994183255458)
XLA Ops:
  0.0 102.1 %panel.1 = bf16[32,2048]{1,0:T(8,128)(2,1)} custom-call(bf16[32,2048]{1,0:T(8,128)(2,1)} %tokens.1, bf16[2048,896]{1,0:T(8,128)(2,1)} %gate.1, bf16[2048,896]{1,0:T(8,128)(2,1)} %up.1, bf16[896,2048]{1,0:T(8,128)(2,1)} %down.1), custom_call_target="tpu_custom_call" | custom-call | tf_op jit(solution)/shard_map/panel/pallas_call | solution.py:378
  102.1 1.6 %copy.6 = bf16[32,2048]{1,0:T(8,128)(2,1)} copy(bf16[32,2048]{1,0:T(8,128)(2,1)} %panel.1) | data formatting | bytes 262144

commit v3 on v2

--- a/solution.py
+++ b/solution.py
@@ -11,32 +11,33 @@
 SPLIT = ((0, 2), (2, 4), (4, 6), (6, 7))
 MEET = ((1, 1, 1, 1), (1, 1, 1, 1), (1, 1, 1, 1), (1, 1, 1, 1))
 GATHER_DIRECT = (1, 1, 1, 1)
-SCATTER_DIRECT = (1, 1, 1, 1)
+SCATTER_DIRECT = (0, 0, 1, 1)
+PROJECT_EARLY = (0, 0, 0, 0)
 SECOND, THIRD = BF16, BF16
 POOL = 48
 PIECES = len(SPLIT)
 
 ORDER = (
-    (0, 0), (1, 0), (0, 1), (1, 3), (2, 0, 0), (2, 0, 1), (1, 1), (1, 2), (2, 3, 1), (2, 3, 0), (4, 0),
-    (5, 0, 1), (5, 0, 0), (6, 0, 1, 0), (5, 0, 2), (2, 1, 0), (6, 0, 0, 0), (2, 1, 1), (6, 0, 2, 0), (5, 0, 3),
-    (6, 0, 1, 1), (4, 3), (5, 3, 0), (5, 3, 3), (2, 2, 0), (6, 0, 3, 0), (2, 2, 1), (5, 3, 1), (6, 0, 2, 1),
-    (6, 3, 0, 0), (5, 3, 2), (6, 0, 3, 1), (6, 3, 1, 0), (4, 1), (5, 1, 0), (6, 0, 0, 1), (6, 3, 3, 0),
-    (5, 1, 2), (5, 1, 1), (6, 0, 1, 2), (7, 0, 1, 3), (6, 3, 2, 0), (6, 1, 0, 0), (6, 3, 0, 1), (5, 1, 3),
-    (4, 2), (5, 2, 1), (6, 3, 1, 1), (6, 0, 2, 2), (6, 0, 0, 2), (6, 0, 3, 2), (5, 2, 3), (6, 1, 1, 0),
-    (6, 3, 0, 2), (7, 0, 0, 3), (6, 3, 3, 1), (5, 2, 0), (6, 1, 3, 0), (6, 3, 1, 2), (6, 1, 2, 0), (5, 2, 2),
-    (7, 0, 0, 1), (7, 0, 3, 1), (7, 0, 2, 1), (7, 0, 1, 1), (7, 0, 1, 0), (7, 0, 3, 0), (6, 3, 2, 1),
-    (7, 3, 0, 1), (7, 3, 0, 0), (7, 0, 3, 3), (6, 1, 0, 1), (7, 0, 0, 0), (7, 0, 2, 0), (7, 0, 2, 3),
-    (8, 0, 0), (6, 1, 1, 1), (6, 1, 3, 1), (6, 3, 3, 2), (7, 3, 3, 3), (6, 3, 2, 2), (7, 3, 2, 1),
-    (6, 1, 0, 2), (7, 3, 1, 1), (6, 2, 0, 0), (6, 1, 2, 1), (8, 0, 1), (7, 3, 0, 3), (6, 2, 2, 0),
-    (6, 2, 3, 0), (6, 2, 1, 0), (7, 3, 2, 0), (7, 3, 2, 3), (6, 1, 1, 2), (7, 3, 1, 3), (7, 3, 3, 1),
-    (6, 1, 3, 2), (7, 3, 3, 0), (6, 1, 2, 2), (7, 3, 1, 0), (7, 1, 0, 1), (7, 1, 0, 0), (8, 3, 0),
-    (6, 2, 0, 1), (6, 2, 3, 1), (6, 2, 2, 1), (7, 1, 1, 3), (8, 3, 1), (7, 1, 1, 1), (7, 1, 2, 3),
-    (7, 1, 1, 0), (7, 1, 3, 1), (7, 1, 0, 3), (6, 2, 1, 1), (6, 2, 0, 2), (10, 0, 1), (6, 2, 3, 2),
-    (6, 2, 2, 2), (7, 1, 3, 3), (7, 2, 3, 3), (6, 2, 1, 2), (7, 2, 2, 3), (7, 1, 2, 1), (7, 1, 2, 0),
-    (7, 1, 3, 0), (7, 2, 0, 3), (8, 1, 0), (7, 2, 1, 3), (8, 1, 1), (7, 2, 3, 1), (7, 2, 3, 0), (7, 2, 0, 1),
-    (7, 2, 2, 1), (7, 2, 0, 0), (7, 2, 2, 0), (7, 2, 1, 1), (7, 2, 1, 0), (8, 2, 0), (10, 1, 0), (8, 2, 1),
-    (10, 1, 1), (10, 2, 0), (10, 3, 0), (11, 1, 0), (11, 1, 1), (10, 0, 0), (10, 2, 1), (11, 2, 0), (11, 2, 1),
-    (10, 3, 1), (11, 0, 1), (11, 3, 0), (11, 0, 0), (11, 3, 1),
+    (0, 0), (1, 0), (2, 0, 1), (2, 0, 0), (0, 1), (1, 1), (1, 2), (4, 0), (5, 0, 2), (2, 1, 1), (2, 1, 0),
+    (5, 0, 0), (6, 0, 0, 0), (5, 0, 1), (6, 0, 0, 1), (6, 0, 2, 0), (6, 0, 2, 1), (1, 3), (2, 2, 1), (5, 0, 3),
+    (2, 2, 0), (4, 1), (5, 1, 3), (6, 0, 1, 0), (5, 1, 0), (5, 1, 2), (6, 0, 0, 2), (6, 0, 3, 0), (5, 1, 1),
+    (6, 0, 1, 1), (7, 0, 0, 3), (2, 3, 1), (2, 3, 0), (6, 1, 0, 0), (6, 0, 3, 1), (6, 1, 0, 1), (6, 1, 2, 0),
+    (6, 1, 2, 1), (6, 1, 3, 0), (6, 0, 2, 2), (6, 1, 3, 1), (4, 2), (5, 2, 0), (5, 2, 2), (6, 1, 1, 0),
+    (6, 1, 1, 1), (5, 2, 3), (6, 0, 1, 2), (5, 2, 1), (6, 1, 0, 2), (7, 1, 0, 3), (7, 0, 2, 1), (6, 0, 3, 2),
+    (4, 3), (5, 3, 0), (6, 1, 2, 2), (7, 0, 2, 3), (6, 2, 2, 0), (5, 3, 1), (7, 0, 1, 1), (7, 1, 0, 1),
+    (6, 2, 2, 1), (6, 2, 0, 0), (7, 1, 2, 3), (6, 1, 3, 2), (7, 1, 3, 3), (6, 2, 3, 0), (7, 0, 1, 3),
+    (6, 2, 1, 0), (5, 3, 3), (7, 0, 3, 1), (6, 1, 1, 2), (7, 1, 1, 3), (5, 3, 2), (7, 1, 2, 1), (6, 2, 2, 2),
+    (7, 2, 2, 3), (6, 3, 1, 0), (6, 3, 3, 0), (6, 2, 3, 1), (6, 2, 3, 2), (6, 3, 0, 0), (7, 1, 2, 0),
+    (7, 1, 0, 0), (6, 2, 0, 1), (7, 1, 3, 1), (7, 0, 0, 1), (6, 3, 2, 0), (7, 1, 1, 1), (7, 1, 1, 0),
+    (7, 0, 3, 3), (6, 2, 0, 2), (6, 2, 1, 1), (6, 2, 1, 2), (7, 0, 0, 0), (7, 1, 3, 0), (8, 1, 0), (8, 1, 1),
+    (7, 2, 1, 3), (7, 0, 2, 0), (7, 2, 0, 3), (7, 0, 3, 0), (7, 2, 3, 3), (7, 0, 1, 0), (8, 0, 0), (8, 0, 1),
+    (6, 3, 1, 1), (7, 2, 2, 1), (6, 3, 3, 1), (6, 3, 3, 2), (6, 3, 1, 2), (7, 2, 0, 1), (7, 2, 1, 1),
+    (7, 2, 3, 1), (6, 3, 0, 1), (6, 3, 0, 2), (7, 2, 2, 0), (6, 3, 2, 1), (9, 1, 0), (6, 3, 2, 2), (9, 1, 1),
+    (7, 2, 0, 0), (7, 2, 1, 0), (7, 2, 3, 0), (8, 2, 0), (8, 2, 1), (7, 3, 3, 3), (9, 0, 1), (7, 3, 2, 3),
+    (9, 0, 0), (7, 3, 1, 1), (7, 3, 1, 0), (7, 3, 3, 1), (7, 3, 0, 1), (7, 3, 1, 3), (7, 3, 0, 3), (10, 1, 0),
+    (10, 1, 1), (7, 3, 3, 0), (7, 3, 2, 1), (7, 3, 2, 0), (10, 2, 0), (10, 2, 1), (7, 3, 0, 0), (8, 3, 0),
+    (8, 3, 1), (11, 1, 0), (11, 2, 1), (11, 1, 1), (11, 2, 0), (10, 0, 1), (10, 0, 0), (10, 3, 0), (10, 3, 1),
+    (11, 0, 0), (11, 0, 1), (11, 3, 0), (11, 3, 1),
 )
 
 
@@ -241,7 +242,8 @@
 
     def hidden_copy(k, j, name):
         block = hid.at[k, core, :, units(j)]
-        arrival = ("share", k) if name == "share" else ("back", k, j)
+        apart = bool(PROJECT_EARLY[k]) and j == PIECES - 1
+        arrival = ("share", k, apart) if name == "share" else ("back", k, j)
         device = {"share": mate, "back": behind, "onward": ahead}[name]
         return net.copy(held[name, k, j], arrival, block, block, device)
 
@@ -304,17 +306,26 @@
             if MEET[k][j]:
                 net.give(held["onward", k, j], hidden_copy(k, j, "onward"), pos == 2)
 
-    def project(k, s):
+    def down_product(k, s, first, last, more):
         if s == 0:
             weight(PIECES)
-            net.arrived(("share", k), hid.at[k, 1 - core], mate)
+            part_of = (k, 1 - core, slice(None), pl.ds(first, last - first))
+            net.arrived(("share", k, more), hid.at[part_of], mate)
 
         @pl.loop(4 * s, 4 * s + 4)
         def _(n):
             cols = pl.ds(pl.multiple_of(n * 256, 256), 256)
-            value = jnp.dot(hid[k].reshape(256, 896), wd[:, cols], preferred_element_type=F32)
-            mix[k, :, :, :, cols] = value.reshape(4, 4, 16, 256)
-
+            value = jnp.dot(
+                hid[k, :, :, first:last].reshape(256, last - first), wd[first:last, cols], preferred_element_type=F32
+            ).reshape(4, 4, 16, 256)
+            mix[k, :, :, :, cols] = mix[k, :, :, :, cols] + value if more else value
+
+    def begin(k, s):
+        down_product(k, s, 0, 128 * SPLIT[-1][0], False)
+
+    def project(k, s):
+        early = PROJECT_EARLY[k]
+        down_product(k, s, 128 * SPLIT[-1][0] if early else 0, 896, bool(early))
         a, b = here[s]
         if SCATTER_DIRECT[k]:
             for i, d in enumerate((1, -1, 2)):
@@ -365,7 +376,7 @@
 
     STEPS = (
         tokens_out, tokens_light, tokens_heavy, tokens_forward, tokens_in, multiply,
-        line, back, project, scatter_sum, scatter_light, scatter_across,
+        line, back, project, scatter_sum, scatter_light, scatter_across, begin,
     )
     for number, *args in ORDER:
         STEPS[number](*args)
@@ -377,7 +388,7 @@
     n = CHUNKS
     return pl.pallas_call(
         kernel,
-        out_shape=jax.ShapeDtypeStruct((32, 2048), BF16),
+        out_shape=pltpu.VMEM((32, 2048), BF16),
         in_specs=[hbm] * 4,
         out_specs=pl.BlockSpec(memory_space=pltpu.VMEM),
         scratch_shapes=[

time: 104 us -> 98.1 us (0.943)
  Pallas kernels: 102 us -> 97.3 us
    pallas_call x1, Pallas kernels: 102 us -> 97.3 us  [on_device(): pl.pallas_call(kernel, out_shape=pltpu.VMEM((32, 2048), BF16), in_specs=[...]
where the time goes in v3:
time: 98.1 us; the launch traced here: 98 us
  Pallas kernels  97.3 us (99%)
    pallas_call x1, Pallas kernels, on_device(): pl.pallas_call(kernel, out_shape=pltpu.VMEM((32, 2048), BF16), in_specs=[...  97.3 us

profile of v3, /device:TPU:1, one launch (start us, length us, event | category | flops | bytes accessed | tf_op | source)
XLA Modules:
  0.0 98.0 jit_solution(13421996844298318580)
XLA Ops:
  0.0 97.3 %panel.1 = bf16[32,2048]{1,0:T(8,128)(2,1)S(1)} custom-call(bf16[32,2048]{1,0:T(8,128)(2,1)} %tokens.1, bf16[2048,896]{1,0:T(8,128)(2,1)} %gate.1, bf16[2048,896]{1,0:T(8,128)(2,1)} %up.1, bf16[896,2048]{1,0:T(8,128)(2,1)} %down.1), custom_call_target="tpu_custom_call" | custom-call | tf_op jit(solution)/shard_map/panel/pallas_call | solution.py:389
  97.3 0.7 copy.6

commit v4 on v2

v4 whole, which is shorter than its diff:
```python
import jax
import jax.numpy as jnp
from jax import lax
from jax.experimental import pallas as pl
from jax.experimental.pallas import tpu as pltpu
from jax.sharding import PartitionSpec as P

F32, BF16 = jnp.float32, jnp.bfloat16
GROUPS = 4
OWN, OTHER, HALF_OF = (0, 3), (1, 2), (0, 0, 1, 1)
CHUNKS = 8
SPLIT = ((0, 4), (4, 7))
MEET = ((1, 1), (1, 1), (1, 1), (1, 1), (1, 1), (1, 1), (1, 1), (1, 1))
POOL = 40
PIECES = len(SPLIT)

ORDER = (
    (0, 1), (0, 0), (1, 0), (1, 3), (2, 1, 0), (2, 1, 1), (1, 2), (2, 0, 1), (2, 0, 0), (4, 1), (5, 1, 1),
    (1, 1), (5, 1, 0), (2, 4, 1), (2, 4, 0), (6, 1, 1, 0), (2, 5, 1), (4, 0), (5, 0, 0), (6, 1, 0, 0),
    (2, 5, 0), (2, 2, 0), (6, 1, 1, 1), (5, 0, 1), (2, 7, 0), (2, 3, 0), (2, 2, 1), (6, 1, 0, 1), (4, 4),
    (2, 3, 1), (6, 0, 0, 0), (5, 4, 1), (5, 4, 0), (6, 1, 1, 2), (2, 7, 1), (6, 0, 0, 1), (4, 5), (6, 0, 1, 0),
    (2, 6, 1), (5, 5, 1), (7, 1, 1, 1), (6, 4, 1, 0), (5, 5, 0), (2, 6, 0), (6, 4, 0, 0), (6, 1, 0, 2), (4, 2),
    (6, 4, 1, 1), (5, 2, 1), (7, 1, 1, 3), (6, 0, 1, 1), (5, 2, 0), (6, 5, 1, 0), (7, 1, 0, 1), (6, 4, 0, 1),
    (4, 3), (5, 3, 0), (6, 0, 0, 2), (5, 3, 1), (6, 5, 0, 0), (6, 4, 1, 2), (6, 2, 0, 0), (7, 1, 0, 3),
    (6, 5, 1, 1), (6, 2, 1, 0), (6, 5, 0, 1), (4, 7), (7, 0, 0, 1), (7, 4, 1, 1), (5, 7, 1), (6, 4, 0, 2),
    (6, 2, 0, 1), (6, 0, 1, 2), (5, 7, 0), (7, 0, 0, 3), (7, 4, 1, 3), (7, 4, 0, 1), (4, 6), (7, 0, 1, 1),
    (6, 2, 1, 1), (6, 5, 1, 2), (7, 1, 1, 0), (7, 4, 0, 3), (5, 6, 1), (5, 6, 0), (7, 5, 1, 1), (7, 0, 1, 3),
    (7, 5, 1, 3), (7, 1, 0, 0), (6, 3, 1, 0), (6, 5, 0, 2), (8, 1, 0), (6, 3, 1, 1), (6, 3, 0, 0),
    (7, 5, 0, 1), (6, 3, 0, 1), (6, 2, 0, 2), (6, 7, 0, 0), (7, 5, 0, 3), (8, 1, 1), (6, 7, 1, 0),
    (7, 2, 0, 3), (6, 2, 1, 2), (7, 0, 0, 0), (7, 2, 0, 1), (6, 6, 1, 0), (6, 7, 0, 1), (6, 6, 0, 0),
    (7, 4, 0, 0), (7, 4, 1, 0), (7, 0, 1, 0), (8, 4, 0), (7, 2, 1, 1), (8, 4, 1), (6, 7, 1, 1), (7, 5, 1, 0),
    (8, 0, 0), (7, 2, 1, 3), (6, 6, 1, 1), (8, 0, 1), (6, 3, 1, 2), (7, 5, 0, 0), (8, 5, 0), (8, 5, 1),
    (6, 3, 0, 2), (7, 3, 1, 1), (7, 3, 1, 3), (6, 6, 0, 1), (7, 3, 0, 1), (6, 7, 0, 2), (7, 2, 0, 0),
    (7, 2, 1, 0), (8, 2, 0), (7, 3, 0, 3), (7, 7, 0, 3), (8, 2, 1), (7, 7, 0, 1), (7, 3, 1, 0), (6, 7, 1, 2),
    (7, 7, 1, 1), (7, 3, 0, 0), (7, 7, 1, 3), (6, 6, 1, 2), (7, 6, 1, 3), (8, 3, 0), (7, 6, 1, 1), (8, 3, 1),
    (7, 7, 0, 0), (6, 6, 0, 2), (10, 2, 0), (7, 6, 0, 1), (10, 2, 1), (7, 7, 1, 0), (8, 7, 0), (8, 7, 1),
    (7, 6, 0, 3), (10, 1, 1), (10, 1, 0), (7, 6, 1, 0), (11, 2, 0), (7, 6, 0, 0), (8, 6, 0), (8, 6, 1),
    (10, 0, 1), (11, 1, 0), (10, 0, 0), (11, 2, 1), (11, 1, 1), (10, 3, 0), (10, 3, 1), (11, 0, 0), (11, 0, 1),
    (11, 3, 0), (11, 3, 1),
)


class Net:
    def __init__(self, send_sem, recv_sem):
        self.send_sem, self.recv_sem = send_sem, recv_sem
        self.arrivals, self.free, self.slots = {}, [], 0

    def take(self):
        if self.slots < POOL:
            self.slots += 1
            return self.slots - 1
        slot, one, when = self.free.pop(0)
        self.wait(one, when)
        return slot

    def give(self, slot, one, when=None):
        self.free.append((slot, one, when))

    def wait(self, one, when):
        if when is None:
            one.wait_send()
        else:
            pl.when(when)(one.wait_send)

    def copy(self, slot, name, src, dst, device):
        number = self.arrivals.setdefault(name, len(self.arrivals))
        return pltpu.make_async_remote_copy(
            src_ref=src,
            dst_ref=dst,
            send_sem=self.send_sem.at[slot],
            recv_sem=self.recv_sem.at[number],
            device_id=device,
            device_id_type=pl.DeviceIdType.MESH,
        )

    def start(self, name, src, dst, device):
        slot = self.take()
        one = self.copy(slot, name, src, dst, device)
        one.start()
        self.give(slot, one)

    def arrived(self, name, dst, device):
        assert name in self.arrivals
        self.copy(0, name, dst, dst, device).wait_recv()

    def finish(self):
        for _, one, when in self.free:
            self.wait(one, when)


ARRIVALS = 110


def kernel(tokens, gate, up, down, out, tok, wgu, wd, part, pair, zs, zr, hid, mix, s1, r1, t1, t1s, r2, t2, z3, local_sem, send_sem, recv_sem):
    dp, tensor = lax.axis_index("dp"), lax.axis_index("tensor")
    x, y, zh = dp // 8, (dp // 2) % 4, dp % 2
    zl, core = tensor // 2, tensor % 2
    pos = jnp.where(core == 0, zl, 3 - zl)
    step = jnp.where(core == 0, 1, -1)

    def plane(dx, dy):
        return ((((x + dx + 4) % 4) * 4 + (y + dy + 4) % 4) * 2 + zh, tensor)

    across = ((x * 4 + y) * 2 + 1 - zh, tensor)
    mate = (dp, zl * 2 + 1 - core)
    ahead = (dp, (zl + step) * 2 + core)
    behind = (dp, (zl - step) * 2 + core)

    def columns(j):
        return pl.ds(256 * SPLIT[j][0], 256 * (SPLIT[j][1] - SPLIT[j][0]))

    def units(j):
        return pl.ds(128 * SPLIT[j][0], 128 * (SPLIT[j][1] - SPLIT[j][0]))

    def own(k):
        return 2 * k + (x + y) % 2, y // 2, y % 2, x // 2

    barrier = pltpu.get_barrier_semaphore()

    def greet(device):
        pl.semaphore_signal(barrier, inc=1, device_id=device, device_id_type=pl.DeviceIdType.MESH)

    mine = [
        pltpu.make_async_copy(tokens.at[pl.ds(16 * h, 16)], tok.at[own(OWN[h])], local_sem.at[h])
        for h in range(2)
    ]
    for one in mine:
        one.start()
    for dx, dy in ((1, 0), (-1, 0), (2, 0), (0, 1), (0, -1), (0, 2)):
        greet(plane(dx, dy))
    greet(across)
    greet(mate)
    pl.when(pos < 3)(lambda: greet(ahead))
    pl.when(pos > 0)(lambda: greet(behind))
    for j in range(PIECES):
        for n in range(*SPLIT[j]):
            for g, ref in enumerate((gate, up)):
                pltpu.make_async_copy(
                    ref.at[:, pl.ds(128 * n, 128)],
                    wgu.at[:, pl.ds(256 * n + 128 * g, 128)],
                    local_sem.at[2 + j],
                ).start()
    weights = [
        pltpu.make_async_copy(wgu.at[:, columns(j)], wgu.at[:, columns(j)], local_sem.at[2 + j])
        for j in range(PIECES)
    ]
    weights.append(pltpu.make_async_copy(down, wd, local_sem.at[2 + PIECES]))
    weights[-1].start()
    unread = set(range(PIECES + 1))

    def weight(j):
        if j in unread:
            unread.remove(j)
            weights[j].wait()

    pl.semaphore_wait(barrier, 8 + jnp.where(pos < 3, 1, 0) + jnp.where(pos > 0, 1, 0))

    net = Net(send_sem, recv_sem)

    def light(s, d):
        return plane(d, 0) if s == 0 else plane(0, d)

    def heavy(s, d):
        return plane(0, d) if s == 0 else plane(d, 0)

    here = ((y, x), (x, y))

    def line_of(ref, q, s, a):
        cols = pl.ds(1024 * s, 1024)
        if s == 0:
            return ref.at[q, a // 2, a % 2, :, :, cols]
        return ref.at[q, :, (q + a) % 2, a // 2, :, cols]

    def tokens_out(h):
        mine[h].wait()
        net.start(("z", h), tok.at[own(OWN[h])], tok.at[own(OTHER[h])], across)

    def tokens_light(k):
        if k in OTHER:
            net.arrived(("z", HALF_OF[k]), tok.at[own(k)], across)
        for s in range(2):
            block = tok.at[(*own(k), slice(None), pl.ds(1024 * s, 1024))]
            for d in (1, -1, 2):
                net.start(("light", k, s), block, block, light(s, d))

    came = set()

    def tokens_heavy(q, s):
        if (q // 2, s) not in came:
            came.add((q // 2, s))
            three = tok.at[pl.ds(0, 3), 0, 0, 0, :, pl.ds(0, 1024)]
            net.arrived(("light", q // 2, s), three, light(s, 1))
        line = line_of(tok, q, s, here[s][0])
        for d in (1, -1, 2):
            net.start(("heavy", q, s), line, line, heavy(s, d))

    def tokens_in(q):
        for s in range(2):
            net.arrived(("heavy", q, s), tok.at[pl.ds(0, 3), :, 0, 0, :, pl.ds(0, 1024)], heavy(s, 1))

    def multiply(k, j):
        weight(j)

        @pl.loop(*SPLIT[j])
        def _(n):
            cols = pl.ds(pl.multiple_of(n * 256, 256), 256)
            value = jnp.dot(tok[k].reshape(128, 2048), wgu[:, cols], preferred_element_type=F32)
            part[k, :, :, cols] = value.reshape(2, 64, 256)

        net.start(("pair", k, j), part.at[k, 1 - core, :, columns(j)], pair.at[k, :, columns(j)], mate)

    def total(k, j, rows, *more):
        cols = columns(j)
        value = part[k, core, rows, cols] + pair[k, rows, cols]
        for ref in more:
            value = value + ref[k, rows, cols].astype(F32)
        return value

    held = {}

    def end(k, j):
        return 2 if MEET[k][j] else 3

    def line_copy(k, j, up):
        src = zs.at[k, :, columns(j)]
        if up:
            return net.copy(held["line", k, j], ("line", k, j), src, zr.at[k, :, columns(j)], ahead)
        return net.copy(held["line", k, j], ("line", k, j), src, src, behind)

    def pass_on(k, j, up, *more):
        @pl.loop(0, 4)
        def _(r):
            rows = pl.ds(pl.multiple_of(r * 16, 16), 16)
            zs[k, rows, columns(j)] = total(k, j, rows, *more).astype(BF16)

        line_copy(k, j, up).start()

    def hidden_copy(k, j, name):
        block = hid.at[k, core, :, units(j)]
        arrival = ("share", k) if name == "share" else ("back", k, j)
        device = {"share": mate, "back": behind, "onward": ahead}[name]
        return net.copy(held[name, k, j], arrival, block, block, device)

    def hidden_out(k, j, *names):
        for name in names:
            hidden_copy(k, j, name).start()

    def activate(k, j, *more):
        @pl.loop(0, 4)
        def _(r):
            rows = pl.ds(pl.multiple_of(r * 16, 16), 16)
            value = total(k, j, rows, *more)
            for n in range(SPLIT[j][1] - SPLIT[j][0]):
                g, u = value[:, 256 * n : 256 * n + 128], value[:, 256 * n + 128 : 256 * n + 256]
                unit = 128 * (SPLIT[j][0] + n)
                hid[k, core, rows, unit : unit + 128] = (g / (1.0 + jnp.exp(-g)) * u).astype(BF16)

    def line(k, j, p):
        if p == 0:
            held["line", k, j] = net.take()
            net.arrived(("pair", k, j), pair.at[k, :, columns(j)], mate)
        if p == end(k, j):
            for name in ("back", "share") + (("onward",) if MEET[k][j] else ()):
                held[name, k, j] = net.take()

        def go():
            if p == 0:
                pass_on(k, j, True)
                return
            if p == end(k, j) and MEET[k][j]:
                net.arrived(("line", k, j), zr.at[pl.ds(0, 2), :, columns(j)], behind)
            else:
                net.arrived(("line", k, j), zr.at[k, :, columns(j)], behind)
            if p < end(k, j):
                pass_on(k, j, True, zr)
            elif MEET[k][j]:
                activate(k, j, zr, zs)
                hidden_out(k, j, "back", "onward", "share")
            else:
                activate(k, j, zr)
                hidden_out(k, j, "back", "share")

        pl.when(pos == p)(go)
        if p == 0 and MEET[k][j]:
            pl.when(pos == 3)(lambda: pass_on(k, j, False))
        if p == end(k, j) - 1:
            net.give(held["line", k, j], line_copy(k, j, True), pos != end(k, j))

    backs = {}

    def back(k, j, p):
        def go():
            net.arrived(("back", k, j), hid.at[k, core, :, units(j)], ahead if p < end(k, j) else behind)
            hidden_out(k, j, *(("back",) if p and p < end(k, j) else ()), "share")

        pl.when(pos == p)(go)
        backs[k, j] = backs.get((k, j), 0) + 1
        if backs[k, j] == 3:
            senders = (pos == 1) | (pos == 2) if MEET[k][j] else pos > 0
            net.give(held["back", k, j], hidden_copy(k, j, "back"), senders)
            net.give(held["share", k, j], hidden_copy(k, j, "share"))
            if MEET[k][j]:
                net.give(held["onward", k, j], hidden_copy(k, j, "onward"), pos == 2)

    def project(q, s):
        if s == 0:
            weight(PIECES)
            net.arrived(("share", q), hid.at[q, 1 - core], mate)

        @pl.loop(4 * s, 4 * s + 4)
        def _(n):
            cols = pl.ds(pl.multiple_of(n * 256, 256), 256)
            value = jnp.dot(hid[q].reshape(128, 896), wd[:, cols], preferred_element_type=F32)
            mix[q, :, :, :, :, cols] = value.reshape(2, 2, 2, 16, 256)

        a, b = here[s]
        for i, d in enumerate((1, -1, 2)):
            s1[q, s, i] = line_of(mix, q, s, (a + d + 4) % 4)[...].astype(BF16)
            net.start(("last", q, s), s1.at[q, s, i], r1.at[q, s, i], heavy(s, d))

    def scatter_light(k, s):
        a, b = here[s]
        for p in range(2):
            q = 2 * k + p
            net.arrived(("last", q, s), r1.at[q, s], heavy(s, 1))
            value = line_of(mix, q, s, a)[...]
            for i in range(3):
                value = value + r1[q, s, i].astype(F32)
            for i in range(2):
                t1[k, s, 2 * i + (p + a) % 2] = value[i]
                t1s[k, s, 2 * i + (p + a) % 2] = value[i].astype(BF16)
        for i, d in enumerate((1, -1, 2)):
            net.start(("second", k, s), t1s.at[k, s, (b + d + 4) % 4], r2.at[k, s, i], light(s, d))

    def scatter_across(k, s):
        a, b = here[s]
        net.arrived(("second", k, s), r2.at[k, s], light(s, 1))
        value = t1[k, s, b]
        for i in range(3):
            value = value + r2[k, s, i].astype(F32)
        h = HALF_OF[k]
        if k in OTHER:
            t2[h, s] = value.astype(BF16)
            net.start(("third", h, s), t2.at[h, s], z3.at[h, s], across)
        else:
            net.arrived(("third", h, s), z3.at[h, s], across)
            out[16 * h : 16 * h + 16, 1024 * s : 1024 * s + 1024] = (value + z3[h, s].astype(F32)).astype(BF16)

    STEPS = (
        tokens_out, tokens_light, tokens_heavy, None, tokens_in, multiply,
        line, back, project, None, scatter_light, scatter_across,
    )
    for number, *args in ORDER:
        STEPS[number](*args)
    net.finish()


def on_device(tokens, gate_weight, up_weight, down_weight):
    hbm = pl.BlockSpec(memory_space=pl.ANY)
    n, g = CHUNKS, GROUPS
    return pl.pallas_call(
        kernel,
        out_shape=pltpu.VMEM((32, 2048), BF16),
        in_specs=[hbm] * 4,
        out_specs=pl.BlockSpec(memory_space=pltpu.VMEM),
        scratch_shapes=[
            pltpu.VMEM((n, 2, 2, 2, 16, 2048), BF16),
            pltpu.VMEM((2048, 1792), BF16),
            pltpu.VMEM((896, 2048), BF16),
            pltpu.VMEM((n, 2, 64, 1792), F32),
            pltpu.VMEM((n, 64, 1792), F32),
            pltpu.VMEM((n, 64, 1792), BF16),
            pltpu.VMEM((n, 64, 1792), BF16),
            pltpu.VMEM((n, 2, 64, 896), BF16),
            pltpu.VMEM((n, 2, 2, 2, 16, 2048), F32),
            pltpu.VMEM((n, 2, 3, 2, 16, 1024), BF16),
            pltpu.VMEM((n, 2, 3, 2, 16, 1024), BF16),
            pltpu.VMEM((g, 2, 4, 16, 1024), F32),
            pltpu.VMEM((g, 2, 4, 16, 1024), BF16),
            pltpu.VMEM((g, 2, 3, 16, 1024), BF16),
            pltpu.VMEM((2, 2, 16, 1024), BF16),
            pltpu.VMEM((2, 2, 16, 1024), BF16),
            pltpu.SemaphoreType.DMA((3 + PIECES,)),
            pltpu.SemaphoreType.DMA((POOL,)),
            pltpu.SemaphoreType.DMA((ARRIVALS,)),
        ],
        compiler_params=pltpu.CompilerParams(
            collective_id=0, has_side_effects=True, vmem_limit_bytes=60 * 2**20
        ),
        name="panel",
    )(tokens, gate_weight, up_weight, down_weight)


def solution(mesh):
    return jax.shard_map(
        on_device,
        mesh=mesh,
        in_specs=(P("dp", "tensor"), P("tensor", "dp"), P("tensor", "dp"), P("dp", "tensor")),
        out_specs=P("dp", "tensor"),
        check_vma=False,
    )
```

time: 104 us -> 92.9 us (0.89)
  Pallas kernels: 102 us -> 92.2 us
    pallas_call x1, Pallas kernels: 102 us -> 92.2 us  [on_device(): pl.pallas_call(kernel, out_shape=pltpu.VMEM((32, 2048), BF16), in_specs=[...]
where the time goes in v4:
time: 92.9 us; the launch traced here: 92.8 us
  Pallas kernels  92.2 us (99%)
    pallas_call x1, Pallas kernels, on_device(): pl.pallas_call(kernel, out_shape=pltpu.VMEM((32, 2048), BF16), in_specs=[...  92.2 us

profile of v4, /device:TPU:1, one launch (start us, length us, event | category | flops | bytes accessed | tf_op | source)
XLA Modules:
  0.0 92.8 jit_solution(11472889988393821965)
XLA Ops:
  0.0 92.2 %panel.1 = bf16[32,2048]{1,0:T(8,128)(2,1)S(1)} custom-call(bf16[32,2048]{1,0:T(8,128)(2,1)} %tokens.1, bf16[2048,896]{1,0:T(8,128)(2,1)} %gate.1, bf16[2048,896]{1,0:T(8,128)(2,1)} %up.1, bf16[896,2048]{1,0:T(8,128)(2,1)} %down.1), custom_call_target="tpu_custom_call" | custom-call | tf_op jit(solution)/shard_map/panel/pallas_call | solution.py:361
  92.2 0.7 copy.6

commit v5 on v4

--- a/solution.py
+++ b/solution.py
@@ -9,34 +9,37 @@
 GROUPS = 4
 OWN, OTHER, HALF_OF = (0, 3), (1, 2), (0, 0, 1, 1)
 CHUNKS = 8
-SPLIT = ((0, 4), (4, 7))
-MEET = ((1, 1), (1, 1), (1, 1), (1, 1), (1, 1), (1, 1), (1, 1), (1, 1))
+SPLIT = (((0, 4), (4, 7)), ((0, 1), (1, 4), (4, 7)), ((0, 4), (4, 7)), ((0, 4), (4, 7)), ((0, 4), (4, 7)), ((0, 4), (4, 7)), ((0, 4), (4, 7)), ((0, 4), (4, 7)))
+EARLY = (0, 7)
+MEET = ((1, 1), (1, 1, 1), (1, 1), (1, 1), (1, 1), (1, 1), (1, 1), (1, 1))
 POOL = 40
-PIECES = len(SPLIT)
+CUTS = sorted({edge for pieces in SPLIT for piece in pieces for edge in piece})
+PARTS = tuple(zip(CUTS, CUTS[1:]))
 
 ORDER = (
-    (0, 1), (0, 0), (1, 0), (1, 3), (2, 1, 0), (2, 1, 1), (1, 2), (2, 0, 1), (2, 0, 0), (4, 1), (5, 1, 1),
-    (1, 1), (5, 1, 0), (2, 4, 1), (2, 4, 0), (6, 1, 1, 0), (2, 5, 1), (4, 0), (5, 0, 0), (6, 1, 0, 0),
-    (2, 5, 0), (2, 2, 0), (6, 1, 1, 1), (5, 0, 1), (2, 7, 0), (2, 3, 0), (2, 2, 1), (6, 1, 0, 1), (4, 4),
-    (2, 3, 1), (6, 0, 0, 0), (5, 4, 1), (5, 4, 0), (6, 1, 1, 2), (2, 7, 1), (6, 0, 0, 1), (4, 5), (6, 0, 1, 0),
-    (2, 6, 1), (5, 5, 1), (7, 1, 1, 1), (6, 4, 1, 0), (5, 5, 0), (2, 6, 0), (6, 4, 0, 0), (6, 1, 0, 2), (4, 2),
-    (6, 4, 1, 1), (5, 2, 1), (7, 1, 1, 3), (6, 0, 1, 1), (5, 2, 0), (6, 5, 1, 0), (7, 1, 0, 1), (6, 4, 0, 1),
-    (4, 3), (5, 3, 0), (6, 0, 0, 2), (5, 3, 1), (6, 5, 0, 0), (6, 4, 1, 2), (6, 2, 0, 0), (7, 1, 0, 3),
-    (6, 5, 1, 1), (6, 2, 1, 0), (6, 5, 0, 1), (4, 7), (7, 0, 0, 1), (7, 4, 1, 1), (5, 7, 1), (6, 4, 0, 2),
-    (6, 2, 0, 1), (6, 0, 1, 2), (5, 7, 0), (7, 0, 0, 3), (7, 4, 1, 3), (7, 4, 0, 1), (4, 6), (7, 0, 1, 1),
-    (6, 2, 1, 1), (6, 5, 1, 2), (7, 1, 1, 0), (7, 4, 0, 3), (5, 6, 1), (5, 6, 0), (7, 5, 1, 1), (7, 0, 1, 3),
-    (7, 5, 1, 3), (7, 1, 0, 0), (6, 3, 1, 0), (6, 5, 0, 2), (8, 1, 0), (6, 3, 1, 1), (6, 3, 0, 0),
-    (7, 5, 0, 1), (6, 3, 0, 1), (6, 2, 0, 2), (6, 7, 0, 0), (7, 5, 0, 3), (8, 1, 1), (6, 7, 1, 0),
-    (7, 2, 0, 3), (6, 2, 1, 2), (7, 0, 0, 0), (7, 2, 0, 1), (6, 6, 1, 0), (6, 7, 0, 1), (6, 6, 0, 0),
-    (7, 4, 0, 0), (7, 4, 1, 0), (7, 0, 1, 0), (8, 4, 0), (7, 2, 1, 1), (8, 4, 1), (6, 7, 1, 1), (7, 5, 1, 0),
-    (8, 0, 0), (7, 2, 1, 3), (6, 6, 1, 1), (8, 0, 1), (6, 3, 1, 2), (7, 5, 0, 0), (8, 5, 0), (8, 5, 1),
-    (6, 3, 0, 2), (7, 3, 1, 1), (7, 3, 1, 3), (6, 6, 0, 1), (7, 3, 0, 1), (6, 7, 0, 2), (7, 2, 0, 0),
-    (7, 2, 1, 0), (8, 2, 0), (7, 3, 0, 3), (7, 7, 0, 3), (8, 2, 1), (7, 7, 0, 1), (7, 3, 1, 0), (6, 7, 1, 2),
-    (7, 7, 1, 1), (7, 3, 0, 0), (7, 7, 1, 3), (6, 6, 1, 2), (7, 6, 1, 3), (8, 3, 0), (7, 6, 1, 1), (8, 3, 1),
-    (7, 7, 0, 0), (6, 6, 0, 2), (10, 2, 0), (7, 6, 0, 1), (10, 2, 1), (7, 7, 1, 0), (8, 7, 0), (8, 7, 1),
-    (7, 6, 0, 3), (10, 1, 1), (10, 1, 0), (7, 6, 1, 0), (11, 2, 0), (7, 6, 0, 0), (8, 6, 0), (8, 6, 1),
-    (10, 0, 1), (11, 1, 0), (10, 0, 0), (11, 2, 1), (11, 1, 1), (10, 3, 0), (10, 3, 1), (11, 0, 0), (11, 0, 1),
-    (11, 3, 0), (11, 3, 1),
+    (0, 1), (0, 0), (1, 0), (1, 3), (2, 1, 0), (2, 1, 1), (1, 2), (1, 1), (4, 1), (5, 1, 0), (2, 5, 1),
+    (2, 5, 0), (5, 1, 2), (2, 4, 1), (2, 4, 0), (6, 1, 0, 0), (2, 3, 1), (5, 1, 1), (2, 3, 0), (2, 2, 1),
+    (6, 1, 0, 1), (6, 1, 2, 0), (2, 2, 0), (4, 5), (5, 5, 1), (6, 1, 1, 0), (6, 1, 2, 1), (5, 5, 0),
+    (6, 5, 1, 0), (2, 6, 0), (2, 6, 1), (2, 7, 1), (2, 7, 0), (2, 0, 0), (4, 4), (5, 4, 1), (6, 5, 0, 0),
+    (6, 1, 1, 1), (6, 5, 1, 1), (5, 4, 0), (2, 0, 1), (6, 5, 0, 1), (6, 1, 2, 2), (6, 1, 0, 2), (4, 3),
+    (5, 3, 0), (6, 4, 1, 0), (5, 3, 1), (6, 4, 1, 1), (4, 2), (6, 4, 0, 0), (7, 1, 2, 3), (5, 2, 0),
+    (6, 5, 1, 2), (6, 1, 1, 2), (5, 2, 1), (4, 6), (6, 3, 1, 0), (6, 3, 0, 0), (6, 4, 0, 1), (4, 7), (5, 6, 0),
+    (6, 5, 0, 2), (6, 3, 1, 1), (5, 7, 0), (6, 2, 0, 0), (6, 4, 1, 2), (5, 6, 1), (7, 1, 1, 3), (7, 5, 1, 3),
+    (6, 3, 0, 1), (6, 2, 1, 0), (7, 1, 2, 1), (4, 0), (7, 1, 0, 3), (5, 0, 0), (6, 4, 0, 2), (7, 5, 0, 1),
+    (5, 7, 1), (7, 5, 1, 1), (7, 5, 0, 3), (7, 4, 1, 3), (7, 4, 1, 1), (6, 3, 1, 2), (7, 1, 1, 1),
+    (7, 3, 1, 3), (7, 4, 0, 3), (6, 2, 0, 1), (6, 7, 0, 0), (5, 0, 1), (6, 3, 0, 2), (6, 6, 0, 0),
+    (7, 5, 0, 0), (6, 6, 1, 0), (6, 7, 1, 0), (6, 2, 1, 1), (7, 5, 1, 0), (8, 5, 0), (7, 4, 0, 1),
+    (7, 4, 1, 0), (6, 2, 0, 2), (8, 5, 1), (6, 7, 0, 1), (6, 0, 0, 0), (7, 3, 1, 1), (7, 4, 0, 0),
+    (7, 1, 0, 1), (6, 0, 1, 0), (7, 3, 0, 3), (7, 1, 1, 0), (6, 2, 1, 2), (7, 3, 0, 1), (8, 4, 0), (8, 4, 1),
+    (7, 3, 1, 0), (7, 3, 0, 0), (6, 6, 0, 1), (7, 2, 0, 1), (7, 2, 1, 3), (7, 1, 2, 0), (6, 7, 0, 2),
+    (7, 2, 0, 3), (6, 6, 1, 1), (8, 3, 0), (7, 2, 1, 1), (8, 3, 1), (6, 6, 0, 2), (6, 7, 1, 1), (7, 2, 0, 0),
+    (6, 6, 1, 2), (7, 7, 0, 3), (7, 2, 1, 0), (8, 2, 0), (7, 6, 1, 3), (10, 2, 0), (7, 1, 0, 0), (6, 0, 0, 1),
+    (10, 2, 1), (7, 7, 0, 1), (6, 7, 1, 2), (6, 0, 1, 1), (8, 2, 1), (7, 6, 0, 1), (7, 6, 0, 3), (8, 1, 0),
+    (7, 6, 1, 1), (6, 0, 0, 2), (8, 1, 1), (7, 7, 0, 0), (6, 0, 1, 2), (7, 6, 0, 0), (7, 0, 0, 3), (10, 1, 0),
+    (7, 7, 1, 3), (7, 6, 1, 0), (7, 7, 1, 1), (8, 6, 0), (8, 6, 1), (7, 0, 0, 1), (10, 1, 1), (7, 7, 1, 0),
+    (12, 7, 0), (7, 0, 1, 1), (7, 0, 1, 3), (11, 2, 1), (12, 7, 1), (8, 7, 0), (7, 0, 0, 0), (8, 7, 1),
+    (12, 0, 0), (11, 2, 0), (7, 0, 1, 0), (12, 0, 1), (8, 0, 0), (8, 0, 1), (11, 1, 0), (11, 1, 1), (10, 3, 0),
+    (10, 3, 1), (10, 0, 0), (10, 0, 1), (11, 3, 0), (11, 3, 1), (11, 0, 0), (11, 0, 1),
 )
 
 
@@ -88,7 +91,7 @@
             self.wait(one, when)
 
 
-ARRIVALS = 110
+ARRIVALS = 115
 
 
 def kernel(tokens, gate, up, down, out, tok, wgu, wd, part, pair, zs, zr, hid, mix, s1, r1, t1, t1s, r2, t2, z3, local_sem, send_sem, recv_sem):
@@ -106,11 +109,14 @@
     ahead = (dp, (zl + step) * 2 + core)
     behind = (dp, (zl - step) * 2 + core)
 
-    def columns(j):
-        return pl.ds(256 * SPLIT[j][0], 256 * (SPLIT[j][1] - SPLIT[j][0]))
-
-    def units(j):
-        return pl.ds(128 * SPLIT[j][0], 128 * (SPLIT[j][1] - SPLIT[j][0]))
+    def tiles(first, last, width):
+        return pl.ds(width * first, width * (last - first))
+
+    def columns(q, j):
+        return tiles(*SPLIT[q][j], 256)
+
+    def units(q, j):
+        return tiles(*SPLIT[q][j], 128)
 
     def own(k):
         return 2 * k + (x + y) % 2, y // 2, y % 2, x // 2
@@ -132,26 +138,29 @@
     greet(mate)
     pl.when(pos < 3)(lambda: greet(ahead))
     pl.when(pos > 0)(lambda: greet(behind))
-    for j in range(PIECES):
-        for n in range(*SPLIT[j]):
-            for g, ref in enumerate((gate, up)):
-                pltpu.make_async_copy(
-                    ref.at[:, pl.ds(128 * n, 128)],
-                    wgu.at[:, pl.ds(256 * n + 128 * g, 128)],
-                    local_sem.at[2 + j],
-                ).start()
-    weights = [
-        pltpu.make_async_copy(wgu.at[:, columns(j)], wgu.at[:, columns(j)], local_sem.at[2 + j])
-        for j in range(PIECES)
-    ]
-    weights.append(pltpu.make_async_copy(down, wd, local_sem.at[2 + PIECES]))
-    weights[-1].start()
-    unread = set(range(PIECES + 1))
-
-    def weight(j):
-        if j in unread:
-            unread.remove(j)
-            weights[j].wait()
+    weights = []
+
+    def load_weights():
+        for i, part_of in enumerate(PARTS):
+            for n in range(*part_of):
+                for g, ref in enumerate((gate, up)):
+                    pltpu.make_async_copy(
+                        ref.at[:, pl.ds(128 * n, 128)],
+                        wgu.at[:, pl.ds(256 * n + 128 * g, 128)],
+                        local_sem.at[2 + i],
+                    ).start()
+            block = wgu.at[:, tiles(*part_of, 256)]
+            weights.append(pltpu.make_async_copy(block, block, local_sem.at[2 + i]))
+        weights.append(pltpu.make_async_copy(down, wd, local_sem.at[2 + len(PARTS)]))
+        weights[-1].start()
+
+    load_weights()
+    unread = set(range(len(weights)))
+
+    def weight(i):
+        if i in unread:
+            unread.remove(i)
+            weights[i].wait()
 
     pl.semaphore_wait(barrier, 8 + jnp.where(pos < 3, 1, 0) + jnp.where(pos > 0, 1, 0))
 
@@ -199,18 +208,20 @@
             net.arrived(("heavy", q, s), tok.at[pl.ds(0, 3), :, 0, 0, :, pl.ds(0, 1024)], heavy(s, 1))
 
     def multiply(k, j):
-        weight(j)
-
-        @pl.loop(*SPLIT[j])
+        for i, (first, _) in enumerate(PARTS):
+            if SPLIT[k][j][0] <= first < SPLIT[k][j][1]:
+                weight(i)
+
+        @pl.loop(*SPLIT[k][j])
         def _(n):
             cols = pl.ds(pl.multiple_of(n * 256, 256), 256)
             value = jnp.dot(tok[k].reshape(128, 2048), wgu[:, cols], preferred_element_type=F32)
             part[k, :, :, cols] = value.reshape(2, 64, 256)
 
-        net.start(("pair", k, j), part.at[k, 1 - core, :, columns(j)], pair.at[k, :, columns(j)], mate)
+        net.start(("pair", k, j), part.at[k, 1 - core, :, columns(k, j)], pair.at[k, :, columns(k, j)], mate)
 
     def total(k, j, rows, *more):
-        cols = columns(j)
+        cols = columns(k, j)
         value = part[k, core, rows, cols] + pair[k, rows, cols]
         for ref in more:
             value = value + ref[k, rows, cols].astype(F32)
@@ -222,22 +233,23 @@
         return 2 if MEET[k][j] else 3
 
     def line_copy(k, j, up):
-        src = zs.at[k, :, columns(j)]
+        src = zs.at[k, :, columns(k, j)]
         if up:
-            return net.copy(held["line", k, j], ("line", k, j), src, zr.at[k, :, columns(j)], ahead)
+            return net.copy(held["line", k, j], ("line", k, j), src, zr.at[k, :, columns(k, j)], ahead)
         return net.copy(held["line", k, j], ("line", k, j), src, src, behind)
 
     def pass_on(k, j, up, *more):
         @pl.loop(0, 4)
         def _(r):
             rows = pl.ds(pl.multiple_of(r * 16, 16), 16)
-            zs[k, rows, columns(j)] = total(k, j, rows, *more).astype(BF16)
+            zs[k, rows, columns(k, j)] = total(k, j, rows, *more).astype(BF16)
 
         line_copy(k, j, up).start()
 
     def hidden_copy(k, j, name):
-        block = hid.at[k, core, :, units(j)]
-        arrival = ("share", k) if name == "share" else ("back", k, j)
+        block = hid.at[k, core, :, units(k, j)]
+        final = k in EARLY and j == len(SPLIT[k]) - 1
+        arrival = ("share", k, final) if name == "share" else ("back", k, j)
         device = {"share": mate, "back": behind, "onward": ahead}[name]
         return net.copy(held[name, k, j], arrival, block, block, device)
 
@@ -250,15 +262,15 @@
         def _(r):
             rows = pl.ds(pl.multiple_of(r * 16, 16), 16)
             value = total(k, j, rows, *more)
-            for n in range(SPLIT[j][1] - SPLIT[j][0]):
+            for n in range(SPLIT[k][j][1] - SPLIT[k][j][0]):
                 g, u = value[:, 256 * n : 256 * n + 128], value[:, 256 * n + 128 : 256 * n + 256]
-                unit = 128 * (SPLIT[j][0] + n)
+                unit = 128 * (SPLIT[k][j][0] + n)
                 hid[k, core, rows, unit : unit + 128] = (g / (1.0 + jnp.exp(-g)) * u).astype(BF16)
 
     def line(k, j, p):
         if p == 0:
             held["line", k, j] = net.take()
-            net.arrived(("pair", k, j), pair.at[k, :, columns(j)], mate)
+            net.arrived(("pair", k, j), pair.at[k, :, columns(k, j)], mate)
         if p == end(k, j):
             for name in ("back", "share") + (("onward",) if MEET[k][j] else ()):
                 held[name, k, j] = net.take()
@@ -268,9 +280,9 @@
                 pass_on(k, j, True)
                 return
             if p == end(k, j) and MEET[k][j]:
-                net.arrived(("line", k, j), zr.at[pl.ds(0, 2), :, columns(j)], behind)
+                net.arrived(("line", k, j), zr.at[pl.ds(0, 2), :, columns(k, j)], behind)
             else:
-                net.arrived(("line", k, j), zr.at[k, :, columns(j)], behind)
+                net.arrived(("line", k, j), zr.at[k, :, columns(k, j)], behind)
             if p < end(k, j):
                 pass_on(k, j, True, zr)
             elif MEET[k][j]:
@@ -290,7 +302,7 @@
 
     def back(k, j, p):
         def go():
-            net.arrived(("back", k, j), hid.at[k, core, :, units(j)], ahead if p < end(k, j) else behind)
+            net.arrived(("back", k, j), hid.at[k, core, :, units(k, j)], ahead if p < end(k, j) else behind)
             hidden_out(k, j, *(("back",) if p and p < end(k, j) else ()), "share")
 
         pl.when(pos == p)(go)
@@ -302,17 +314,25 @@
             if MEET[k][j]:
                 net.give(held["onward", k, j], hidden_copy(k, j, "onward"), pos == 2)
 
-    def project(q, s):
+    def down_product(q, s, first, last, more):
         if s == 0:
-            weight(PIECES)
-            net.arrived(("share", q), hid.at[q, 1 - core], mate)
+            weight(len(PARTS))
+            net.arrived(("share", q, more), hid.at[q, 1 - core, :, pl.ds(first, last - first)], mate)
 
         @pl.loop(4 * s, 4 * s + 4)
         def _(n):
             cols = pl.ds(pl.multiple_of(n * 256, 256), 256)
-            value = jnp.dot(hid[q].reshape(128, 896), wd[:, cols], preferred_element_type=F32)
-            mix[q, :, :, :, :, cols] = value.reshape(2, 2, 2, 16, 256)
-
+            value = jnp.dot(
+                hid[q, :, :, first:last].reshape(128, last - first), wd[first:last, cols], preferred_element_type=F32
+            ).reshape(2, 2, 2, 16, 256)
+            mix[q, :, :, :, :, cols] = mix[q, :, :, :, :, cols] + value if more else value
+
+    def begin(q, s):
+        down_product(q, s, 0, 128 * SPLIT[q][-1][0], False)
+
+    def project(q, s):
+        early = q in EARLY
+        down_product(q, s, 128 * SPLIT[q][-1][0] if early else 0, 896, early)
         a, b = here[s]
         for i, d in enumerate((1, -1, 2)):
             s1[q, s, i] = line_of(mix, q, s, (a + d + 4) % 4)[...].astype(BF16)
@@ -348,7 +368,7 @@
 
     STEPS = (
         tokens_out, tokens_light, tokens_heavy, None, tokens_in, multiply,
-        line, back, project, None, scatter_light, scatter_across,
+        line, back, project, None, scatter_light, scatter_across, begin,
     )
     for number, *args in ORDER:
         STEPS[number](*args)
@@ -380,7 +400,7 @@
             pltpu.VMEM((g, 2, 3, 16, 1024), BF16),
             pltpu.VMEM((2, 2, 16, 1024), BF16),
             pltpu.VMEM((2, 2, 16, 1024), BF16),
-            pltpu.SemaphoreType.DMA((3 + PIECES,)),
+            pltpu.SemaphoreType.DMA((3 + len(PARTS),)),
             pltpu.SemaphoreType.DMA((POOL,)),
             pltpu.SemaphoreType.DMA((ARRIVALS,)),
         ],

time: 92.9 us -> 92.1 us (level)
  no operation moved by 1% of the time
where the time goes in v5:
time: 92.1 us; the launch traced here: 92 us
  Pallas kernels  91.4 us (99%)
    pallas_call x1, Pallas kernels, on_device(): pl.pallas_call(kernel, out_shape=pltpu.VMEM((32, 2048), BF16), in_specs=[...  91.4 us

profile of v5, /device:TPU:1, one launch (start us, length us, event | category | flops | bytes accessed | tf_op | source)
XLA Modules:
  0.0 92.0 jit_solution(6085616690191023418)
XLA Ops:
  0.0 91.4 %panel.1 = bf16[32,2048]{1,0:T(8,128)(2,1)S(1)} custom-call(bf16[32,2048]{1,0:T(8,128)(2,1)} %tokens.1, bf16[2048,896]{1,0:T(8,128)(2,1)} %gate.1, bf16[2048,896]{1,0:T(8,128)(2,1)} %up.1, bf16[896,2048]{1,0:T(8,128)(2,1)} %down.1), custom_call_target="tpu_custom_call" | custom-call | tf_op jit(solution)/shard_map/panel/pallas_call | solution.py:381
  91.4 0.7 copy.6

commit v6 on v5

--- a/solution.py
+++ b/solution.py
@@ -17,8 +17,8 @@
 PARTS = tuple(zip(CUTS, CUTS[1:]))
 
 ORDER = (
-    (0, 1), (0, 0), (1, 0), (1, 3), (2, 1, 0), (2, 1, 1), (1, 2), (1, 1), (4, 1), (5, 1, 0), (2, 5, 1),
-    (2, 5, 0), (5, 1, 2), (2, 4, 1), (2, 4, 0), (6, 1, 0, 0), (2, 3, 1), (5, 1, 1), (2, 3, 0), (2, 2, 1),
+    (0, 1), (1, 0), (1, 3), (2, 1, 0), (2, 1, 1), (0, 0), (1, 2), (4, 1), (5, 1, 0), (2, 5, 1),
+    (2, 5, 0), (5, 1, 2), (1, 1), (2, 4, 1), (2, 4, 0), (6, 1, 0, 0), (2, 3, 1), (5, 1, 1), (2, 3, 0), (2, 2, 1),
     (6, 1, 0, 1), (6, 1, 2, 0), (2, 2, 0), (4, 5), (5, 5, 1), (6, 1, 1, 0), (6, 1, 2, 1), (5, 5, 0),
     (6, 5, 1, 0), (2, 6, 0), (2, 6, 1), (2, 7, 1), (2, 7, 0), (2, 0, 0), (4, 4), (5, 4, 1), (6, 5, 0, 0),
     (6, 1, 1, 1), (6, 5, 1, 1), (5, 4, 0), (2, 0, 1), (6, 5, 0, 1), (6, 1, 2, 2), (6, 1, 0, 2), (4, 3),
@@ -180,13 +180,22 @@
             return ref.at[q, a // 2, a % 2, :, :, cols]
         return ref.at[q, :, (q + a) % 2, a // 2, :, cols]
 
+    unheld = {0, 1}
+
+    def hold(h):
+        if h in unheld:
+            unheld.remove(h)
+            mine[h].wait()
+
     def tokens_out(h):
-        mine[h].wait()
+        hold(h)
         net.start(("z", h), tok.at[own(OWN[h])], tok.at[own(OTHER[h])], across)
 
     def tokens_light(k):
         if k in OTHER:
             net.arrived(("z", HALF_OF[k]), tok.at[own(k)], across)
+        else:
+            hold(HALF_OF[k])
         for s in range(2):
             block = tok.at[(*own(k), slice(None), pl.ds(1024 * s, 1024))]
             for d in (1, -1, 2):

time: 92.1 us -> 94.3 us (1.024)
  Pallas kernels: 91.4 us -> 93.6 us
    pallas_call x1, Pallas kernels: 91.4 us -> 93.6 us  [on_device(): pl.pallas_call(kernel, out_shape=pltpu.VMEM((32, 2048), BF16), in_specs=[...]
where the time goes in v6:
time: 94.3 us; the launch traced here: 94.2 us
  Pallas kernels  93.6 us (99%)
    pallas_call x1, Pallas kernels, on_device(): pl.pallas_call(kernel, out_shape=pltpu.VMEM((32, 2048), BF16), in_specs=[...  93.6 us

profile of v6, /device:TPU:1, one launch (start us, length us, event | category | flops | bytes accessed | tf_op | source)
XLA Modules:
  0.0 94.2 jit_solution(18105671387389432398)
XLA Ops:
  0.0 93.6 %panel.1 = bf16[32,2048]{1,0:T(8,128)(2,1)S(1)} custom-call(bf16[32,2048]{1,0:T(8,128)(2,1)} %tokens.1, bf16[2048,896]{1,0:T(8,128)(2,1)} %gate.1, bf16[2048,896]{1,0:T(8,128)(2,1)} %up.1, bf16[896,2048]{1,0:T(8,128)(2,1)} %down.1), custom_call_target="tpu_custom_call" | custom-call | tf_op jit(solution)/shard_map/panel/pallas_call | solution.py:390
  93.6 0.7 copy.6
